TPU v7x, 128 devices: a whole 4x4x4 slice. The times are simulated.
128 devices in a mesh: gx: 4 (over x), gy: 32 (over z, y, core).
Axes of the slice: x: 4, y: 4, z: 4, core: 2. Of those that a mesh axis runs over, the one named last changes fastest.
Arguments:
- fields: float32 [256, 6, 32, 1024], P(('gx', 'gy')), may hold values from -6 to 6
- speeds: float32 [256, 3, 32, 1024], P(('gx', 'gy')), may hold values from -0.4 to 0.4
- neighbours: int32 [256, 6], replicated, may hold values from -1 to 255, as said below
- block_order: int32 [256], replicated, may hold values from 0 to 255, as said below
- tiles: float32 [16384, 8, 128], P(('gx', 'gy')), may hold values from -6 to 6
- tile_fill: int32 [16384], P(('gx', 'gy')), may hold values from 1 to 128
- tile_dest: int32 [16384, 1], P(('gx', 'gy')), may hold values from 0 to 127; in each aligned block of 128 rows (0 to 127, 128 to 255, ...) at most 2 rows name the same one
Outputs:
- blocks_out: float32 [256, 6, 32, 1024], P(('gx', 'gy'))
- tiles_out: float32 [32768, 8, 128], P(('gx', 'gy'))
- fill_out: int32 [32768], P(('gx', 'gy'))
Inputs may be any that keep to these rules, and one draw needn't show every extreme that they name: Entries 2 d and 2 d + 1 of a row name the blocks below and above along direction d, or -1 at the domain's edge; the relation is symmetric; a block b stands on device b // 2, and each of its neighbours on a device at most 2 away. A permutation; block_order[j] // 2 differs from j // 2 by at most 1, and by 1 for some j. `tile_dest`: among the 128 tiles of one device, no destination is named more than 2 times.
All inputs are finite; a program needn't handle non-finite values.
Results may differ from a plain program's by a relative error of at most 0.0003.
Values sent between devices are 32-bit elements; how exact they have to be, the bound alone decides.
A program may use at most 128 MiB of HBM per device.

v0:
```python
import jax
import jax.numpy as jnp
from jax import lax
from jax.sharding import PartitionSpec as P

NF = 6
CAPT = 2
NEAR = 2


DRIFT = 0.5


def shifted(block, axis, distance):
    devices = range(lax.axis_size(axis))
    route = [(i - distance, i) for i in devices if i - distance in devices]
    return lax.ppermute(block, axis, route)


def directional(values, velocity, direction):
    width = values.shape[2]
    joined = jnp.concatenate([values, velocity[:, direction : direction + 1]], axis=1)
    joined = joined.reshape(joined.shape[0], joined.shape[1], width, width, width)
    joined = jnp.moveaxis(joined, 2 + direction, 2)
    return joined.reshape(joined.shape[0], joined.shape[1], width, width * width)


def restore(swept, direction):
    width = swept.shape[2]
    cube = swept.reshape(swept.shape[0], swept.shape[1], width, width, width)
    cube = jnp.moveaxis(cube, 2, 2 + direction)
    return cube.reshape(swept.shape[0], swept.shape[1], width, width * width)


def face_layers(joined):
    return jnp.stack([joined[:, :, :3], joined[:, :, -3:]], axis=1)


def ppm_update(values, courant):
    width = values.shape[2] - 6
    left_cell = values[:, :, 1:-2]
    right_cell = values[:, :, 2:-1]
    edges = 7.0 / 12.0 * (left_cell + right_cell) - 1.0 / 12.0 * (
        values[:, :, :-3] + values[:, :, 3:]
    )
    edges = jnp.clip(edges, jnp.minimum(left_cell, right_cell), jnp.maximum(left_cell, right_cell))
    centre = values[:, :, 2 : width + 4]
    lower = edges[:, :, : width + 2]
    upper = edges[:, :, 1 : width + 3]
    level = (upper - centre) * (centre - lower) <= 0.0
    lower = jnp.where(level, centre, lower)
    upper = jnp.where(level, centre, upper)
    spread = upper - lower
    tilt = spread * (centre - 0.5 * (lower + upper))
    bound = spread * spread / 6.0
    new_lower = jnp.where(tilt > bound, 3.0 * centre - 2.0 * upper, lower)
    new_upper = jnp.where(tilt < -bound, 3.0 * centre - 2.0 * lower, upper)
    spread = new_upper - new_lower
    curve = 6.0 * (centre - 0.5 * (new_lower + new_upper))
    backward = -courant
    from_left = courant * (
        new_upper[:, :, :-1]
        - 0.5 * courant * (spread[:, :, :-1] - (1.0 - courant * (2.0 / 3.0)) * curve[:, :, :-1])
    )
    from_right = courant * (
        new_lower[:, :, 1:]
        + 0.5 * backward * (spread[:, :, 1:] + (1.0 - backward * (2.0 / 3.0)) * curve[:, :, 1:])
    )
    flux = jnp.where(courant > 0.0, from_left, from_right)
    return values[:, :, 3 : width + 3] - (flux[:, :, 1:] - flux[:, :, :-1])


def sweep_blocks(joined, lower_ghost, upper_ghost, lower_id, upper_id):
    edge_low = jnp.broadcast_to(joined[:, :, :1], lower_ghost.shape)
    edge_high = jnp.broadcast_to(joined[:, :, -1:], upper_ghost.shape)
    lower = jnp.where((lower_id >= 0)[:, None, None, None], lower_ghost, edge_low)
    upper = jnp.where((upper_id >= 0)[:, None, None, None], upper_ghost, edge_high)
    extended = jnp.concatenate([lower, joined, upper], axis=2)
    fields_num = joined.shape[1] - 1
    width = joined.shape[2]
    return ppm_update(extended[:, :fields_num], extended[:, fields_num:, 3 : width + 4])


def pool_index(block_ids, locate, device_now, per_device, reach):
    spots = locate[jnp.maximum(block_ids, 0)]
    index_pool = (spots // per_device - device_now + reach) * per_device + spots % per_device
    return jnp.clip(index_pool, 0, (2 * reach + 1) * per_device - 1)


def gather_ghosts(layers, reach):
    pieces = []
    for offset in range(-reach, reach + 1):
        if offset == 0:
            pieces.append(layers)
        else:
            pieces.append(shifted(layers, ("gx", "gy"), -offset))
    return jnp.concatenate(pieces, axis=0)


def advance(values, velocity, links, locate, device_now, reach):
    per_device = values.shape[0]
    for direction in range(3):
        joined = directional(values, velocity, direction)
        pooled = gather_ghosts(face_layers(joined), reach)
        lower_id = links[:, 2 * direction]
        upper_id = links[:, 2 * direction + 1]
        lower_ghost = pooled[pool_index(lower_id, locate, device_now, per_device, reach), 1]
        upper_ghost = pooled[pool_index(upper_id, locate, device_now, per_device, reach), 0]
        swept = sweep_blocks(joined, lower_ghost, upper_ghost, lower_id, upper_id)
        values = restore(swept, direction)
    return values


def relocate(stacked, incoming, device_now):
    per_device = stacked.shape[0]
    received = [shifted(stacked, ("gx", "gy"), offset) for offset in (1, -1)]
    pooled = jnp.concatenate([received[0], stacked, received[1]], axis=0)
    picks = (incoming // per_device - device_now + 1) * per_device + incoming % per_device
    return jnp.take(pooled, picks, axis=0)


def body(fields, speeds, neighbours, block_order, tiles, tile_fill, tile_dest):
    per_device = fields.shape[0]
    total_blocks = block_order.shape[0]
    device_now = lax.axis_index(("gx", "gy"))
    first_block = device_now * per_device
    incoming = lax.dynamic_slice_in_dim(block_order, first_block, per_device)
    stacked = jnp.concatenate([fields, speeds], axis=1)
    arrived_blocks = relocate(stacked, incoming, device_now)
    placement_new = (
        jnp.zeros((total_blocks,), jnp.int32)
        .at[block_order]
        .set(jnp.arange(total_blocks, dtype=jnp.int32))
    )
    links = jnp.take(neighbours, incoming, axis=0)
    blocks_out = advance(
        arrived_blocks[:, :NF], arrived_blocks[:, NF:], links, placement_new, device_now, NEAR + 2
    )
    devices = lax.axis_size(("gx", "gy"))
    records = jnp.arange(tiles.shape[2], dtype=jnp.int32)
    live_mask = records[None, :] < tile_fill[:, None]
    drifted = jnp.concatenate([tiles[:, 0:3] + DRIFT * tiles[:, 3:6], tiles[:, 3:]], axis=1)
    drifted = jnp.where(live_mask[:, None, :], drifted, 0.0)
    target = tile_dest[:, 0]
    onehot = (target[:, None] == jnp.arange(devices, dtype=jnp.int32)[None, :]).astype(jnp.int32)
    ranking = jnp.sum((jnp.cumsum(onehot, axis=0) - onehot) * onehot, axis=1)
    slot_index = target * CAPT + ranking
    outgoing = (
        jnp.zeros((devices * CAPT, tiles.shape[1], tiles.shape[2]), tiles.dtype)
        .at[slot_index]
        .set(drifted)
    )
    out_fills = jnp.zeros((devices * CAPT,), jnp.int32).at[slot_index].set(tile_fill)
    tiles_out, fill_out = (
        lax.all_to_all(outgoing, ("gx", "gy"), split_axis=0, concat_axis=0, tiled=True),
        lax.all_to_all(out_fills, ("gx", "gy"), split_axis=0, concat_axis=0, tiled=True),
    )
    return (blocks_out, tiles_out, fill_out)


def solution(mesh):
    placed = (
        P(("gx", "gy"), None, None, None),
        P(("gx", "gy"), None, None, None),
        P(),
        P(),
        P(("gx", "gy"), None, None),
        P(("gx", "gy")),
        P(("gx", "gy"), None),
    )
    return jax.shard_map(
        body,
        mesh=mesh,
        in_specs=placed,
        out_specs=(P(("gx", "gy"), None, None, None), P(("gx", "gy"), None, None), P(("gx", "gy"))),
        check_vma=False,
    )
```

profile of v0, /device:TPU:112, one launch (start us, length us, event | category | flops | bytes accessed | tf_op | source)
XLA Modules:
  0.0 371.6 jit_solution(17171845198595484602)
XLA Ops:
  2.4 2.1 collective-permute-start
  4.4 3.6 collective-permute-start.1
  10.3 10.2 %all-to-all-start.1 = ((s32[128,2,1]{1,2,0:T(1,128)}), s32[128,2,1]{1,2,0:T(1,128)}, u32[]{:S(2)}, u32[]{:S(2)}) async-start(s32[128,2,1]{1,2,0:T(1,128)} %bitcast.44), calls=%async_computation.1 | async-start | bytes 131072 | tf_op jit(solution)/shard_map/all_to_all | solution.py:156
  30.1 13.2 %scatter_fusion = f32[256,8,128]{2,1,0:T(8,128)} fusion(f32[256,8,128]{2,1,0:T(8,128)} %broadcast_in_dim.191, s32[128]{0:T(128)S(1)} %fusion.80, f32[128,8,128]{2,1,0:T(8,128)S(1)} %maximum_select_fusion), kind=kCustom, calls=%fused_computation.15 | custom fusion | bytes 1573376 | tf_op jit(solution)/shard_map/scatter | solution.py:151
  43.7 4.9 %pad_maximum_fusion = f32[6,9,32,1024]{3,2,1,0:T(8,128)} fusion(f32[2,9,32,1024]{3,2,1,0:T(8,128)} %collective-permute-done.1, f32[2,9,32,1024]{3,2,1,0:T(8,128)S(1)} %constant_dynamic-update-slice_fusion, f32[2,9,32,1024]{3,2,1,0:T(8,128)} %collective-permute-done), kind=kLoop, calls=%fused_computation.18 | loop fusion | flops 3538944 | bytes 14155776 | tf_op jit(solution)/shard_map/concatenate | solution.py:117
  48.7 3.7 gather_fusion
  52.9 2.6 collective-permute-start.2
  55.5 3.5 collective-permute-start.3
  59.0 4.0 %collective-permute-start.4 = (f32[2,2,7,3,1024]{4,3,2,0,1:T(4,128)S(1)}, f32[2,2,7,3,1024]{4,3,2,0,1:T(4,128)S(1)}, u32[]{:S(2)}, u32[]{:S(2)}) collective-permute-start(f32[2,2,7,3,1024]{4,3,2,0,1:T(4,128)S(1)} %pad_maximum_fusion.11), channel_id=1, source_target_pairs={{0,2},{1,3},{2,4},{3,5},{4,6},{5,7},{6,8},{7,9},{8,10},{9,11},{10,... | collective-permute-start | bytes 1032200 | tf_op jit(solution)/shard_map/ppermute | solution.py:17
  63.0 2.3 collective-permute-start.5
  65.3 3.2 collective-permute-start.6
  69.8 3.1 collective-permute-start.7
  73.1 4.9 %collective-permute-done.3 = f32[2,2,7,3,1024]{4,3,2,0,1:T(4,128)S(1)} collective-permute-done((f32[2,2,7,3,1024]{4,3,2,0,1:T(4,128)S(1)}, f32[2,2,7,3,1024]{4,3,2,0,1:T(4,128)S(1)}, u32[]{:S(2)}, u32[]{:S(2)}) %collective-permute-start.3) | collective-permute-done | bytes 344096 | tf_op jit(solution)/shard_map/ppermute | solution.py:17
  78.0 8.2 %collective-permute-start.8 = (f32[2,2,7,3,1024]{4,3,2,0,1:T(4,128)S(1)}, f32[2,2,7,3,1024]{4,3,2,0,1:T(4,128)S(1)}, u32[]{:S(2)}, u32[]{:S(2)}) collective-permute-start(f32[2,2,7,3,1024]{4,3,2,0,1:T(4,128)S(1)} %pad_maximum_fusion.11), channel_id=1, source_target_pairs={{3,0},{4,1},{5,2},{6,3},{7,4},{8,5},{9,6},{10,7},{11,8},{12,9},{13... | collective-permute-start | bytes 1032200 | tf_op jit(solution)/shard_map/ppermute | solution.py:17
  86.3 10.1 %collective-permute-done.4 = f32[2,2,7,3,1024]{4,3,2,0,1:T(4,128)S(1)} collective-permute-done((f32[2,2,7,3,1024]{4,3,2,0,1:T(4,128)S(1)}, f32[2,2,7,3,1024]{4,3,2,0,1:T(4,128)S(1)}, u32[]{:S(2)}, u32[]{:S(2)}) %collective-permute-start.4) | collective-permute-done | bytes 344096 | tf_op jit(solution)/shard_map/ppermute | solution.py:17
  96.4 3.7 %collective-permute-start.9 = (f32[2,2,7,3,1024]{4,3,2,0,1:T(4,128)S(1)}, f32[2,2,7,3,1024]{4,3,2,0,1:T(4,128)S(1)}, u32[]{:S(2)}, u32[]{:S(2)}) collective-permute-start(f32[2,2,7,3,1024]{4,3,2,0,1:T(4,128)S(1)} %pad_maximum_fusion.11), channel_id=1, source_target_pairs={{4,0},{5,1},{6,2},{7,3},{8,4},{9,5},{10,6},{11,7},{12,8},{13,9},{1... | collective-permute-start | bytes 1032200 | tf_op jit(solution)/shard_map/ppermute | solution.py:17
  101.0 12.5 %collective-permute-done.9 = f32[2,2,7,3,1024]{4,3,2,0,1:T(4,128)S(1)} collective-permute-done((f32[2,2,7,3,1024]{4,3,2,0,1:T(4,128)S(1)}, f32[2,2,7,3,1024]{4,3,2,0,1:T(4,128)S(1)}, u32[]{:S(2)}, u32[]{:S(2)}) %collective-permute-start.9) | collective-permute-done | bytes 344096 | tf_op jit(solution)/shard_map/ppermute | solution.py:17
  113.6 1.9 copy-done.9
  115.5 2.9 gather_fusion.3
  119.5 3.5 gather_fusion.5
  125.4 1.8 fusion.87
  130.9 4.6 %reshape.653 = f32[2,7,32,32,32]{4,3,2,1,0:T(8,128)} reshape(f32[2,7,32,1024]{3,2,1,0:T(8,128)S(1)} %pad_maximum_fusion.10) | data formatting | bytes 3670016 | tf_op jit(solution)/shard_map/reshape | solution.py:23
  135.5 11.5 %copy.93 = f32[2,7,32,32,32]{4,3,2,1,0:T(8,128)} copy(f32[2,7,32,32,32]{4,2,3,1,0:T(8,128)} %bitcast.95) | data formatting | bytes 3670016 | tf_op jit(solution)/shard_map/transpose | solution.py:24
  147.0 5.8 %reshape.654 = f32[2,7,32,1024]{3,2,1,0:T(8,128)S(1)} reshape(f32[2,7,32,32,32]{4,3,2,1,0:T(8,128)} %copy.93) | data formatting | bytes 3670016 | tf_op jit(solution)/shard_map/reshape | solution.py:25
  153.9 1.9 collective-permute-start.10
  159.0 1.9 collective-permute-start.11
  160.9 1.9 collective-permute-start.12
  162.8 3.0 collective-permute-start.13
  165.9 2.5 collective-permute-start.14
  168.9 3.7 collective-permute-start.15
  173.7 1.7 collective-permute-done.11
  175.5 3.9 %collective-permute-start.16 = (f32[2,2,7,3,1024]{4,3,2,0,1:T(4,128)}, f32[2,2,7,3,1024]{4,3,2,0,1:T(4,128)S(1)}, u32[]{:S(2)}, u32[]{:S(2)}) collective-permute-start(f32[2,2,7,3,1024]{4,3,2,0,1:T(4,128)} %pad_maximum_fusion.12), channel_id=1, source_target_pairs={{3,0},{4,1},{5,2},{6,3},{7,4},{8,5},{9,6},{10,7},{11,8},{12,9},{13... | collective-permute-start | bytes 1032200 | tf_op jit(solution)/shard_map/ppermute | solution.py:17
  179.5 15.4 %collective-permute-done.12 = f32[2,2,7,3,1024]{4,3,2,0,1:T(4,128)S(1)} collective-permute-done((f32[2,2,7,3,1024]{4,3,2,0,1:T(4,128)}, f32[2,2,7,3,1024]{4,3,2,0,1:T(4,128)S(1)}, u32[]{:S(2)}, u32[]{:S(2)}) %collective-permute-start.12) | collective-permute-done | bytes 344096 | tf_op jit(solution)/shard_map/ppermute | solution.py:17
  194.9 2.4 collective-permute-start.17
  198.1 21.4 %collective-permute-done.17 = f32[2,2,7,3,1024]{4,3,2,0,1:T(4,128)S(1)} collective-permute-done((f32[2,2,7,3,1024]{4,3,2,0,1:T(4,128)}, f32[2,2,7,3,1024]{4,3,2,0,1:T(4,128)S(1)}, u32[]{:S(2)}, u32[]{:S(2)}) %collective-permute-start.17) | collective-permute-done | bytes 344096 | tf_op jit(solution)/shard_map/ppermute | solution.py:17
  219.6 1.9 copy-done.10
  221.5 2.9 gather_fusion.7
  225.4 3.5 gather_fusion.9
  231.4 1.8 fusion.86
  234.1 2.6 fusion.18
  236.8 9.2 %all-to-all-start = ((f32[256,8,128]{2,1,0:T(8,128)}), f32[256,8,128]{2,1,0:T(8,128)}, u32[]{:S(2)}, u32[]{:S(2)}) async-start(f32[256,8,128]{2,1,0:T(8,128)} %scatter_fusion), calls=%async_computation | async-start | bytes 2097152 | tf_op jit(solution)/shard_map/all_to_all | solution.py:155
  246.0 2.6 fusion.49
  248.5 4.1 %reshape.655 = f32[2,6,32,32,32]{4,3,2,1,0:T(8,128)} reshape(f32[2,6,32,1024]{3,2,1,0:T(8,128)S(1)} %fusion.49) | data formatting | bytes 3145728 | tf_op jit(solution)/shard_map/reshape | solution.py:30
  252.6 8.9 %copy.106 = f32[2,6,32,32,32]{2,3,4,1,0:T(8,128)} copy(f32[2,6,32,32,32]{4,3,2,1,0:T(8,128)} %reshape.655) | data formatting | bytes 3145728 | tf_op jit(solution)/shard_map/reshape | solution.py:30
  261.5 6.9 %maximum_bitcast_fusion = f32[2,7,32,32,32]{4,3,2,1,0:T(8,128)} fusion(f32[2,1,32,32,32]{3,2,4,1,0:T(8,128)S(1)} %copy-done.2, f32[2,6,32,32,32]{3,2,4,1,0:T(8,128)} %bitcast.96), kind=kLoop, calls=%fused_computation.17 | loop fusion | flops 458752 | bytes 3670016 | tf_op jit(solution)/shard_map/transpose | solution.py:24
  268.4 5.8 %reshape.656 = f32[2,7,32,1024]{3,2,1,0:T(8,128)S(1)} reshape(f32[2,7,32,32,32]{4,3,2,1,0:T(8,128)} %maximum_bitcast_fusion) | data formatting | bytes 3670016 | tf_op jit(solution)/shard_map/reshape | solution.py:25
  274.4 2.6 collective-permute-start.18
  280.0 3.4 collective-permute-start.19
  283.4 4.0 %collective-permute-start.20 = (f32[2,2,7,3,1024]{4,3,2,0,1:T(4,128)S(1)}, f32[2,2,7,3,1024]{4,3,2,0,1:T(4,128)S(1)}, u32[]{:S(2)}, u32[]{:S(2)}) collective-permute-start(f32[2,2,7,3,1024]{4,3,2,0,1:T(4,128)S(1)} %pad_maximum_fusion.13), channel_id=1, source_target_pairs={{0,2},{1,3},{2,4},{3,5},{4,6},{5,7},{6,8},{7,9},{8,10},{9,11},{10,... | collective-permute-start | bytes 1032200 | tf_op jit(solution)/shard_map/ppermute | solution.py:17
  287.4 2.3 collective-permute-start.21
  289.8 3.2 collective-permute-start.22
  293.3 1.9 collective-permute-start.23
  295.3 4.1 %collective-permute-done.19 = f32[2,2,7,3,1024]{4,3,2,0,1:T(4,128)S(1)} collective-permute-done((f32[2,2,7,3,1024]{4,3,2,0,1:T(4,128)S(1)}, f32[2,2,7,3,1024]{4,3,2,0,1:T(4,128)S(1)}, u32[]{:S(2)}, u32[]{:S(2)}) %collective-permute-start.19) | collective-permute-done | bytes 344096 | tf_op jit(solution)/shard_map/ppermute | solution.py:17
  299.4 8.2 %collective-permute-start.24 = (f32[2,2,7,3,1024]{4,3,2,0,1:T(4,128)S(1)}, f32[2,2,7,3,1024]{4,3,2,0,1:T(4,128)S(1)}, u32[]{:S(2)}, u32[]{:S(2)}) collective-permute-start(f32[2,2,7,3,1024]{4,3,2,0,1:T(4,128)S(1)} %pad_maximum_fusion.13), channel_id=1, source_target_pairs={{3,0},{4,1},{5,2},{6,3},{7,4},{8,5},{9,6},{10,7},{11,8},{12,9},{13... | collective-permute-start | bytes 1032200 | tf_op jit(solution)/shard_map/ppermute | solution.py:17
  307.8 10.1 %collective-permute-done.20 = f32[2,2,7,3,1024]{4,3,2,0,1:T(4,128)S(1)} collective-permute-done((f32[2,2,7,3,1024]{4,3,2,0,1:T(4,128)S(1)}, f32[2,2,7,3,1024]{4,3,2,0,1:T(4,128)S(1)}, u32[]{:S(2)}, u32[]{:S(2)}) %collective-permute-start.20) | collective-permute-done | bytes 344096 | tf_op jit(solution)/shard_map/ppermute | solution.py:17
  317.9 3.8 %collective-permute-start.25 = (f32[2,2,7,3,1024]{4,3,2,0,1:T(4,128)S(1)}, f32[2,2,7,3,1024]{4,3,2,0,1:T(4,128)S(1)}, u32[]{:S(2)}, u32[]{:S(2)}) collective-permute-start(f32[2,2,7,3,1024]{4,3,2,0,1:T(4,128)S(1)} %pad_maximum_fusion.13), channel_id=1, source_target_pairs={{4,0},{5,1},{6,2},{7,3},{8,4},{9,5},{10,6},{11,7},{12,8},{13,9},{1... | collective-permute-start | bytes 1032200 | tf_op jit(solution)/shard_map/ppermute | solution.py:17
  322.5 20.2 %collective-permute-done.25 = f32[2,2,7,3,1024]{4,3,2,0,1:T(4,128)S(1)} collective-permute-done((f32[2,2,7,3,1024]{4,3,2,0,1:T(4,128)S(1)}, f32[2,2,7,3,1024]{4,3,2,0,1:T(4,128)S(1)}, u32[]{:S(2)}, u32[]{:S(2)}) %collective-permute-start.25) | collective-permute-done | bytes 344096 | tf_op jit(solution)/shard_map/ppermute | solution.py:17
  342.8 1.9 copy-done.11
  344.7 2.9 gather_fusion.11
  348.7 3.5 gather_fusion.13
  354.6 1.8 fusion.85
  359.2 4.0 %copy.122 = f32[2,6,32,1024]{2,3,1,0:T(8,128)} copy(f32[2,6,32,1024]{3,2,1,0:T(8,128)S(1)} %fusion.48) | data formatting | bytes 3145728 | tf_op jit(solution)/shard_map/reshape | solution.py:30
  363.2 5.9 %reshape.658 = f32[2,6,32,1024]{3,2,1,0:T(8,128)} reshape(f32[2,6,32,32,32]{4,3,2,1,0:T(8,128)} %bitcast.97) | data formatting | bytes 3145728 | tf_op jit(solution)/shard_map/reshape | solution.py:32
  369.1 2.3 copy.160
  (178 shorter events, 45.6 us)
Async XLA Ops:
  0.6 1.6 copy-start.8
  0.6 7.4 %copy-start.14 = (s32[128,1]{0,1:T(1,128)S(1)}, s32[128,1]{0,1:T(1,128)}, u32[]{:S(2)}) copy-start(s32[128,1]{0,1:T(1,128)} %param.13) | copy-start | bytes 1540
  0.7 7.9 %copy-start.17 = (s32[128]{0:T(128)S(1)}, s32[128]{0:T(128)}, u32[]{:S(2)}) copy-start(s32[128]{0:T(128)} %param.12) | copy-start | bytes 1540
  0.7 19.9 %copy-start.12 = (s32[256,6]{0,1:T(8,128)S(1)}, s32[256,6]{0,1:T(8,128)}, u32[]{:S(2)}) copy-start(s32[256,6]{0,1:T(8,128)} %param.9) | copy-start | bytes 18436
  0.7 20.0 %copy-start.13 = (s32[256]{0:T(256)S(1)}, s32[256]{0:T(256)}, u32[]{:S(2)}) copy-start(s32[256]{0:T(256)} %param.10) | copy-start | bytes 3076
  2.4 26.3 %copy-start.3 = (f32[128,8,128]{2,1,0:T(8,128)S(1)}, f32[128,8,128]{2,1,0:T(8,128)}, u32[]{:S(2)}) copy-start(f32[128,8,128]{2,1,0:T(8,128)} %param.11) | copy-start | bytes 1572868
  2.4 41.3 %collective-permute-start = (f32[2,9,32,1024]{3,2,1,0:T(8,128)S(1)}, f32[2,9,32,1024]{3,2,1,0:T(8,128)}, u32[]{:S(2)}, u32[]{:S(2)}) collective-permute-start(f32[2,9,32,1024]{3,2,1,0:T(8,128)S(1)} %constant_dynamic-update-slice_fusion), channel_id=1, source_target_pairs={{0,1},{1,2},{2,3},{3,4},{4,5},{5,6},{6,7},{7,8},{8,9},{9,10},{10,1... | collective-permute-start | bytes 7077896 | tf_op jit(solution)/shard_map/ppermute | solution.py:17
  4.4 39.3 %collective-permute-start.1 = (f32[2,9,32,1024]{3,2,1,0:T(8,128)S(1)}, f32[2,9,32,1024]{3,2,1,0:T(8,128)}, u32[]{:S(2)}, u32[]{:S(2)}) collective-permute-start(f32[2,9,32,1024]{3,2,1,0:T(8,128)S(1)} %constant_dynamic-update-slice_fusion), channel_id=1, source_target_pairs={{1,0},{2,1},{3,2},{4,3},{5,4},{6,5},{7,6},{8,7},{9,8},{10,9},{11,1... | collective-permute-start | bytes 7077896 | tf_op jit(solution)/shard_map/ppermute | solution.py:17
  10.3 226.5 %all-to-all-start.1 = ((s32[128,2,1]{1,2,0:T(1,128)}), s32[128,2,1]{1,2,0:T(1,128)}, u32[]{:S(2)}, u32[]{:S(2)}) async-start(s32[128,2,1]{1,2,0:T(1,128)} %bitcast.44), calls=%async_computation.1 | async-start | bytes 131072 | tf_op jit(solution)/shard_map/all_to_all | solution.py:156
  52.7 17.1 %copy-start = (f32[2,9,32,1024]{3,2,1,0:T(8,128)}, f32[2,9,32,1024]{3,2,1,0:T(8,128)S(1)}, u32[]{:S(2)}) copy-start(f32[2,9,32,1024]{3,2,1,0:T(8,128)S(1)} %broadcast_select_fusion) | copy-start | bytes 7077892
  52.9 16.9 %collective-permute-start.2 = (f32[2,2,7,3,1024]{4,3,2,0,1:T(4,128)S(1)}, f32[2,2,7,3,1024]{4,3,2,0,1:T(4,128)S(1)}, u32[]{:S(2)}, u32[]{:S(2)}) collective-permute-start(f32[2,2,7,3,1024]{4,3,2,0,1:T(4,128)S(1)} %pad_maximum_fusion.11), channel_id=1, source_target_pairs={{0,4},{1,5},{2,6},{3,7},{4,8},{5,9},{6,10},{7,11},{8,12},{9,13},{1... | collective-permute-start | bytes 1032200 | tf_op jit(solution)/shard_map/ppermute | solution.py:17
  55.5 22.5 %collective-permute-start.3 = (f32[2,2,7,3,1024]{4,3,2,0,1:T(4,128)S(1)}, f32[2,2,7,3,1024]{4,3,2,0,1:T(4,128)S(1)}, u32[]{:S(2)}, u32[]{:S(2)}) collective-permute-start(f32[2,2,7,3,1024]{4,3,2,0,1:T(4,128)S(1)} %pad_maximum_fusion.11), channel_id=1, source_target_pairs={{0,3},{1,4},{2,5},{3,6},{4,7},{5,8},{6,9},{7,10},{8,11},{9,12},{10... | collective-permute-start | bytes 1032200 | tf_op jit(solution)/shard_map/ppermute | solution.py:17
  59.0 37.5 %collective-permute-start.4 = (f32[2,2,7,3,1024]{4,3,2,0,1:T(4,128)S(1)}, f32[2,2,7,3,1024]{4,3,2,0,1:T(4,128)S(1)}, u32[]{:S(2)}, u32[]{:S(2)}) collective-permute-start(f32[2,2,7,3,1024]{4,3,2,0,1:T(4,128)S(1)} %pad_maximum_fusion.11), channel_id=1, source_target_pairs={{0,2},{1,3},{2,4},{3,5},{4,6},{5,7},{6,8},{7,9},{8,10},{9,11},{10,... | collective-permute-start | bytes 1032200 | tf_op jit(solution)/shard_map/ppermute | solution.py:17
  63.0 37.3 %collective-permute-start.5 = (f32[2,2,7,3,1024]{4,3,2,0,1:T(4,128)S(1)}, f32[2,2,7,3,1024]{4,3,2,0,1:T(4,128)S(1)}, u32[]{:S(2)}, u32[]{:S(2)}) collective-permute-start(f32[2,2,7,3,1024]{4,3,2,0,1:T(4,128)S(1)} %pad_maximum_fusion.11), channel_id=1, source_target_pairs={{0,1},{1,2},{2,3},{3,4},{4,5},{5,6},{6,7},{7,8},{8,9},{9,10},{10,1... | collective-permute-start | bytes 1032200 | tf_op jit(solution)/shard_map/ppermute | solution.py:17
  65.3 35.3 %collective-permute-start.6 = (f32[2,2,7,3,1024]{4,3,2,0,1:T(4,128)S(1)}, f32[2,2,7,3,1024]{4,3,2,0,1:T(4,128)S(1)}, u32[]{:S(2)}, u32[]{:S(2)}) collective-permute-start(f32[2,2,7,3,1024]{4,3,2,0,1:T(4,128)S(1)} %pad_maximum_fusion.11), channel_id=1, source_target_pairs={{1,0},{2,1},{3,2},{4,3},{5,4},{6,5},{7,6},{8,7},{9,8},{10,9},{11,1... | collective-permute-start | bytes 1032200 | tf_op jit(solution)/shard_map/ppermute | solution.py:17
  69.8 30.9 %collective-permute-start.7 = (f32[2,2,7,3,1024]{4,3,2,0,1:T(4,128)S(1)}, f32[2,2,7,3,1024]{4,3,2,0,1:T(4,128)S(1)}, u32[]{:S(2)}, u32[]{:S(2)}) collective-permute-start(f32[2,2,7,3,1024]{4,3,2,0,1:T(4,128)S(1)} %pad_maximum_fusion.11), channel_id=1, source_target_pairs={{2,0},{3,1},{4,2},{5,3},{6,4},{7,5},{8,6},{9,7},{10,8},{11,9},{12,... | collective-permute-start | bytes 1032200 | tf_op jit(solution)/shard_map/ppermute | solution.py:17
  78.0 22.9 %collective-permute-start.8 = (f32[2,2,7,3,1024]{4,3,2,0,1:T(4,128)S(1)}, f32[2,2,7,3,1024]{4,3,2,0,1:T(4,128)S(1)}, u32[]{:S(2)}, u32[]{:S(2)}) collective-permute-start(f32[2,2,7,3,1024]{4,3,2,0,1:T(4,128)S(1)} %pad_maximum_fusion.11), channel_id=1, source_target_pairs={{3,0},{4,1},{5,2},{6,3},{7,4},{8,5},{9,6},{10,7},{11,8},{12,9},{13... | collective-permute-start | bytes 1032200 | tf_op jit(solution)/shard_map/ppermute | solution.py:17
  96.4 17.0 %collective-permute-start.9 = (f32[2,2,7,3,1024]{4,3,2,0,1:T(4,128)S(1)}, f32[2,2,7,3,1024]{4,3,2,0,1:T(4,128)S(1)}, u32[]{:S(2)}, u32[]{:S(2)}) collective-permute-start(f32[2,2,7,3,1024]{4,3,2,0,1:T(4,128)S(1)} %pad_maximum_fusion.11), channel_id=1, source_target_pairs={{4,0},{5,1},{6,2},{7,3},{8,4},{9,5},{10,6},{11,7},{12,8},{13,9},{1... | collective-permute-start | bytes 1032200 | tf_op jit(solution)/shard_map/ppermute | solution.py:17
  113.6 1.9 copy-start.9
  127.2 1.0 copy-start.4
  128.2 1.7 copy-start.1
  129.8 0.9 copy-start.7
  147.0 8.8 %copy-start.15 = (s32[2,1]{1,0:T(2,128)S(1)}, s32[2,1]{1,0:T(2,128)}, u32[]{:S(2)}) copy-start(s32[2,1]{1,0:T(2,128)} %copy.100) | copy-start | bytes 28
  147.0 8.8 %copy-start.16 = (s32[2,1]{1,0:T(2,128)S(1)}, s32[2,1]{1,0:T(2,128)}, u32[]{:S(2)}) copy-start(s32[2,1]{1,0:T(2,128)} %copy.94) | copy-start | bytes 28
  153.9 15.1 %collective-permute-start.10 = (f32[2,2,7,3,1024]{4,3,2,0,1:T(4,128)}, f32[2,2,7,3,1024]{4,3,2,0,1:T(4,128)}, u32[]{:S(2)}, u32[]{:S(2)}) collective-permute-start(f32[2,2,7,3,1024]{4,3,2,0,1:T(4,128)} %pad_maximum_fusion.12), channel_id=1, source_target_pairs={{0,4},{1,5},{2,6},{3,7},{4,8},{5,9},{6,10},{7,11},{8,12},{9,13},{1... | collective-permute-start | bytes 1032200 | tf_op jit(solution)/shard_map/ppermute | solution.py:17
  159.0 16.5 %collective-permute-start.11 = (f32[2,2,7,3,1024]{4,3,2,0,1:T(4,128)}, f32[2,2,7,3,1024]{4,3,2,0,1:T(4,128)S(1)}, u32[]{:S(2)}, u32[]{:S(2)}) collective-permute-start(f32[2,2,7,3,1024]{4,3,2,0,1:T(4,128)} %pad_maximum_fusion.12), channel_id=1, source_target_pairs={{0,3},{1,4},{2,5},{3,6},{4,7},{5,8},{6,9},{7,10},{8,11},{9,12},{10... | collective-permute-start | bytes 1032200 | tf_op jit(solution)/shard_map/ppermute | solution.py:17
  160.9 33.9 %collective-permute-start.12 = (f32[2,2,7,3,1024]{4,3,2,0,1:T(4,128)}, f32[2,2,7,3,1024]{4,3,2,0,1:T(4,128)S(1)}, u32[]{:S(2)}, u32[]{:S(2)}) collective-permute-start(f32[2,2,7,3,1024]{4,3,2,0,1:T(4,128)} %pad_maximum_fusion.12), channel_id=1, source_target_pairs={{0,2},{1,3},{2,4},{3,5},{4,6},{5,7},{6,8},{7,9},{8,10},{9,11},{10,... | collective-permute-start | bytes 1032200 | tf_op jit(solution)/shard_map/ppermute | solution.py:17
  162.8 34.5 %collective-permute-start.13 = (f32[2,2,7,3,1024]{4,3,2,0,1:T(4,128)}, f32[2,2,7,3,1024]{4,3,2,0,1:T(4,128)S(1)}, u32[]{:S(2)}, u32[]{:S(2)}) collective-permute-start(f32[2,2,7,3,1024]{4,3,2,0,1:T(4,128)} %pad_maximum_fusion.12), channel_id=1, source_target_pairs={{0,1},{1,2},{2,3},{3,4},{4,5},{5,6},{6,7},{7,8},{8,9},{9,10},{10,1... | collective-permute-start | bytes 1032200 | tf_op jit(solution)/shard_map/ppermute | solution.py:17
  165.9 31.8 %collective-permute-start.14 = (f32[2,2,7,3,1024]{4,3,2,0,1:T(4,128)}, f32[2,2,7,3,1024]{4,3,2,0,1:T(4,128)S(1)}, u32[]{:S(2)}, u32[]{:S(2)}) collective-permute-start(f32[2,2,7,3,1024]{4,3,2,0,1:T(4,128)} %pad_maximum_fusion.12), channel_id=1, source_target_pairs={{1,0},{2,1},{3,2},{4,3},{5,4},{6,5},{7,6},{8,7},{9,8},{10,9},{11,1... | collective-permute-start | bytes 1032200 | tf_op jit(solution)/shard_map/ppermute | solution.py:17
  168.9 28.9 %collective-permute-start.15 = (f32[2,2,7,3,1024]{4,3,2,0,1:T(4,128)}, f32[2,2,7,3,1024]{4,3,2,0,1:T(4,128)S(1)}, u32[]{:S(2)}, u32[]{:S(2)}) collective-permute-start(f32[2,2,7,3,1024]{4,3,2,0,1:T(4,128)} %pad_maximum_fusion.12), channel_id=1, source_target_pairs={{2,0},{3,1},{4,2},{5,3},{6,4},{7,5},{8,6},{9,7},{10,8},{11,9},{12,... | collective-permute-start | bytes 1032200 | tf_op jit(solution)/shard_map/ppermute | solution.py:17
  175.5 22.5 %collective-permute-start.16 = (f32[2,2,7,3,1024]{4,3,2,0,1:T(4,128)}, f32[2,2,7,3,1024]{4,3,2,0,1:T(4,128)S(1)}, u32[]{:S(2)}, u32[]{:S(2)}) collective-permute-start(f32[2,2,7,3,1024]{4,3,2,0,1:T(4,128)} %pad_maximum_fusion.12), channel_id=1, source_target_pairs={{3,0},{4,1},{5,2},{6,3},{7,4},{8,5},{9,6},{10,7},{11,8},{12,9},{13... | collective-permute-start | bytes 1032200 | tf_op jit(solution)/shard_map/ppermute | solution.py:17
  194.9 24.6 %collective-permute-start.17 = (f32[2,2,7,3,1024]{4,3,2,0,1:T(4,128)}, f32[2,2,7,3,1024]{4,3,2,0,1:T(4,128)S(1)}, u32[]{:S(2)}, u32[]{:S(2)}) collective-permute-start(f32[2,2,7,3,1024]{4,3,2,0,1:T(4,128)} %pad_maximum_fusion.12), channel_id=1, source_target_pairs={{4,0},{5,1},{6,2},{7,3},{8,4},{9,5},{10,6},{11,7},{12,8},{13,9},{1... | collective-permute-start | bytes 1032200 | tf_op jit(solution)/shard_map/ppermute | solution.py:17
  219.5 1.9 copy-start.10
  233.1 1.0 copy-start.6
  236.8 43.2 %all-to-all-start = ((f32[256,8,128]{2,1,0:T(8,128)}), f32[256,8,128]{2,1,0:T(8,128)}, u32[]{:S(2)}, u32[]{:S(2)}) async-start(f32[256,8,128]{2,1,0:T(8,128)} %scatter_fusion), calls=%async_computation | async-start | bytes 2097152 | tf_op jit(solution)/shard_map/all_to_all | solution.py:155
  252.6 8.9 %copy-start.2 = (f32[2,1,32,32,32]{3,2,4,1,0:T(8,128)S(1)}, f32[2,1,32,32,32]{3,2,4,1,0:T(8,128)}, u32[]{:S(2)}) copy-start(f32[2,1,32,32,32]{3,2,4,1,0:T(8,128)} %copy.107) | copy-start | bytes 786436
  274.4 18.9 %collective-permute-start.18 = (f32[2,2,7,3,1024]{4,3,2,0,1:T(4,128)S(1)}, f32[2,2,7,3,1024]{4,3,2,0,1:T(4,128)S(1)}, u32[]{:S(2)}, u32[]{:S(2)}) collective-permute-start(f32[2,2,7,3,1024]{4,3,2,0,1:T(4,128)S(1)} %pad_maximum_fusion.13), channel_id=1, source_target_pairs={{0,4},{1,5},{2,6},{3,7},{4,8},{5,9},{6,10},{7,11},{8,12},{9,13},{1... | collective-permute-start | bytes 1032200 | tf_op jit(solution)/shard_map/ppermute | solution.py:17
  280.0 19.4 %collective-permute-start.19 = (f32[2,2,7,3,1024]{4,3,2,0,1:T(4,128)S(1)}, f32[2,2,7,3,1024]{4,3,2,0,1:T(4,128)S(1)}, u32[]{:S(2)}, u32[]{:S(2)}) collective-permute-start(f32[2,2,7,3,1024]{4,3,2,0,1:T(4,128)S(1)} %pad_maximum_fusion.13), channel_id=1, source_target_pairs={{0,3},{1,4},{2,5},{3,6},{4,7},{5,8},{6,9},{7,10},{8,11},{9,12},{10... | collective-permute-start | bytes 1032200 | tf_op jit(solution)/shard_map/ppermute | solution.py:17
  283.4 34.4 %collective-permute-start.20 = (f32[2,2,7,3,1024]{4,3,2,0,1:T(4,128)S(1)}, f32[2,2,7,3,1024]{4,3,2,0,1:T(4,128)S(1)}, u32[]{:S(2)}, u32[]{:S(2)}) collective-permute-start(f32[2,2,7,3,1024]{4,3,2,0,1:T(4,128)S(1)} %pad_maximum_fusion.13), channel_id=1, source_target_pairs={{0,2},{1,3},{2,4},{3,5},{4,6},{5,7},{6,8},{7,9},{8,10},{9,11},{10,... | collective-permute-start | bytes 1032200 | tf_op jit(solution)/shard_map/ppermute | solution.py:17
  287.4 34.4 %collective-permute-start.21 = (f32[2,2,7,3,1024]{4,3,2,0,1:T(4,128)S(1)}, f32[2,2,7,3,1024]{4,3,2,0,1:T(4,128)S(1)}, u32[]{:S(2)}, u32[]{:S(2)}) collective-permute-start(f32[2,2,7,3,1024]{4,3,2,0,1:T(4,128)S(1)} %pad_maximum_fusion.13), channel_id=1, source_target_pairs={{0,1},{1,2},{2,3},{3,4},{4,5},{5,6},{6,7},{7,8},{8,9},{9,10},{10,1... | collective-permute-start | bytes 1032200 | tf_op jit(solution)/shard_map/ppermute | solution.py:17
  289.8 32.4 %collective-permute-start.22 = (f32[2,2,7,3,1024]{4,3,2,0,1:T(4,128)S(1)}, f32[2,2,7,3,1024]{4,3,2,0,1:T(4,128)S(1)}, u32[]{:S(2)}, u32[]{:S(2)}) collective-permute-start(f32[2,2,7,3,1024]{4,3,2,0,1:T(4,128)S(1)} %pad_maximum_fusion.13), channel_id=1, source_target_pairs={{1,0},{2,1},{3,2},{4,3},{5,4},{6,5},{7,6},{8,7},{9,8},{10,9},{11,1... | collective-permute-start | bytes 1032200 | tf_op jit(solution)/shard_map/ppermute | solution.py:17
  293.3 29.0 %collective-permute-start.23 = (f32[2,2,7,3,1024]{4,3,2,0,1:T(4,128)S(1)}, f32[2,2,7,3,1024]{4,3,2,0,1:T(4,128)S(1)}, u32[]{:S(2)}, u32[]{:S(2)}) collective-permute-start(f32[2,2,7,3,1024]{4,3,2,0,1:T(4,128)S(1)} %pad_maximum_fusion.13), channel_id=1, source_target_pairs={{2,0},{3,1},{4,2},{5,3},{6,4},{7,5},{8,6},{9,7},{10,8},{11,9},{12,... | collective-permute-start | bytes 1032200 | tf_op jit(solution)/shard_map/ppermute | solution.py:17
  299.4 23.0 %collective-permute-start.24 = (f32[2,2,7,3,1024]{4,3,2,0,1:T(4,128)S(1)}, f32[2,2,7,3,1024]{4,3,2,0,1:T(4,128)S(1)}, u32[]{:S(2)}, u32[]{:S(2)}) collective-permute-start(f32[2,2,7,3,1024]{4,3,2,0,1:T(4,128)S(1)} %pad_maximum_fusion.13), channel_id=1, source_target_pairs={{3,0},{4,1},{5,2},{6,3},{7,4},{8,5},{9,6},{10,7},{11,8},{12,9},{13... | collective-permute-start | bytes 1032200 | tf_op jit(solution)/shard_map/ppermute | solution.py:17
  317.9 24.8 %collective-permute-start.25 = (f32[2,2,7,3,1024]{4,3,2,0,1:T(4,128)S(1)}, f32[2,2,7,3,1024]{4,3,2,0,1:T(4,128)S(1)}, u32[]{:S(2)}, u32[]{:S(2)}) collective-permute-start(f32[2,2,7,3,1024]{4,3,2,0,1:T(4,128)S(1)} %pad_maximum_fusion.13), channel_id=1, source_target_pairs={{4,0},{5,1},{6,2},{7,3},{8,4},{9,5},{10,6},{11,7},{12,8},{13,9},{1... | collective-permute-start | bytes 1032200 | tf_op jit(solution)/shard_map/ppermute | solution.py:17
  342.8 1.9 copy-start.11
  356.4 1.0 copy-start.5
where the time goes:
time: 379 us; the launch traced here: 372 us
  local copies, waits for them, and re-layouts  118 us (31%)
  starting transfers between devices  107 us (28%)
  waiting for transfers between devices  101 us (27%)
  other arithmetic  44.3 us (12%)
    ppermute x26, waiting for transfers between devices, shifted(): return lax.ppermute(block, axis, route)  101 us
    ppermute x26, starting transfers between devices, shifted(): return lax.ppermute(block, axis, route)  87.1 us
    reshape x3, local copies, waits for them, and re-layouts, restore(): cube = swept.reshape(swept.shape[0], swept.shape[1], width, width, width)  16.9 us
    unnamed x60, local copies, waits for them, and re-layouts  14.5 us
    scatter x1, local copies, waits for them, and re-layouts, body(): outgoing = jnp.zeros((devices * CAPT, tiles.shape[1], tiles.shape[2]), ti...  13.2 us
    reshape x2, local copies, waits for them, and re-layouts, directional(): joined.reshape(joined.shape[0], joined.shape[1], width, width * width)  11.6 us
    transpose x1, local copies, waits for them, and re-layouts, directional(): joined = jnp.moveaxis(joined, 2 + direction, 2)  11.5 us
    gather x3, local copies, waits for them, and re-layouts, advance(): pooled[pool_index(lower_id, locate, device_now, per_device, reach), 1]  10.6 us
  transfers between devices with their start and end apart: 28, of which 10 were waited for; matrix products, arithmetic and copies ran while one was open for 34% of the time, Pallas kernels for 0%

commit v1 on v0

v1 whole, which is shorter than its diff:
```python
import functools

import jax
import jax.numpy as jnp
from jax import lax
from jax.experimental import pallas as pl
from jax.experimental.pallas import tpu as pltpu
from jax.sharding import PartitionSpec as P

MESH = pl.DeviceIdType.MESH
NF = 6
NB = 2
CAPT = 2
DRIFT = 0.5
AXES = ("gx", "gy")


def pack_kernel(inverse, fills, tiles, out):
    lane = lax.broadcasted_iota(jnp.int32, (3, 128), 1)
    lane5 = lax.broadcasted_iota(jnp.int32, (5, 128), 1)

    def step(slot, carry):
        tile = inverse[slot]
        fill = fills[slot]
        head = tiles[tile, 0:3] + DRIFT * tiles[tile, 3:6]
        out[slot, 0:3] = jnp.where(lane < fill, head, 0.0)
        out[slot, 3:8] = jnp.where(lane5 < fill, tiles[tile, 3:8], 0.0)
        return carry

    lax.fori_loop(0, out.shape[0], step, 0, unroll=8)


def pack_tiles(tiles, inverse, fills, slots):
    return pl.pallas_call(
        pack_kernel,
        out_shape=jax.ShapeDtypeStruct((slots,) + tiles.shape[1:], tiles.dtype),
        in_specs=[
            pl.BlockSpec(memory_space=pltpu.SMEM),
            pl.BlockSpec(memory_space=pltpu.SMEM),
            pl.BlockSpec(memory_space=pltpu.VMEM),
        ],
        out_specs=pl.BlockSpec(memory_space=pltpu.VMEM),
        name="pack_tiles",
    )(inverse, fills, tiles)


def first_two(match, fill):
    width = match.shape[1]
    index = lax.broadcasted_iota(jnp.int32, match.shape, 1)
    first = jnp.min(jnp.where(match, index, width), axis=1)
    last = jnp.max(jnp.where(match, index, -1), axis=1)
    first_fill = jnp.sum(jnp.where(index == first[:, None], fill, 0), axis=1)
    second = jnp.where(last > first, last, width)
    second_fill = jnp.sum(jnp.where(index == second[:, None], fill, 0), axis=1)
    where = jnp.stack([first, second], axis=1).reshape(-1)
    return jnp.minimum(where, width - 1), jnp.stack([first_fill, second_fill], axis=1).reshape(-1)


def ppm(cells, courant):
    delta = [cells[i + 1] - cells[i] for i in range(9)]
    right, left = {}, {}
    for i in range(1, 8):
        step = 0.5 * delta[i] + (1.0 / 12.0) * (delta[i - 1] - delta[i + 1])
        step = jnp.minimum(
            jnp.maximum(step, jnp.minimum(delta[i], 0.0)), jnp.maximum(delta[i], 0.0)
        )
        right[i], left[i + 1] = step, delta[i] - step
    up, down = {}, {}
    for i in range(2, 8):
        r, l = right[i], left[i]
        r2, l2 = r + r, l + l
        up[i] = jnp.maximum(jnp.minimum(r, l2), 0.0) + jnp.minimum(jnp.maximum(r, l2), 0.0)
        down[i] = jnp.maximum(jnp.minimum(l, r2), 0.0) + jnp.minimum(jnp.maximum(l, r2), 0.0)
    flux = []
    for f in range(5):
        c, ca, cb = courant[f]
        a, b = f + 2, f + 3
        wind = c > 0.0
        flux.append(
            c * jnp.where(wind, cells[a], cells[b])
            + ca * jnp.where(wind, up[a], down[b])
            + cb * jnp.where(wind, down[a], up[b])
        )
    return [cells[r + 3] - (flux[r + 1] - flux[r]) for r in range(4)]


def coefficients(c):
    size = jnp.abs(c)
    rest = 1.0 - size
    side = size * rest
    return c, side * rest, side * size


def chosen(flag, shape, ghost, edge):
    return jnp.where(jnp.full(shape, flag, jnp.int32) != 0, ghost, edge)


def advance_kernel(devices, row, sel, fields, speeds, out, *scratch):
    (F, S, T, ST, O, SP0, SP1, SP2, C0, C1, C2), rest = scratch[:11], scratch[11:]
    pools = [rest[6 * s : 6 * s + 6] for s in range(3)]
    R = rest[18:24]
    (in_sem, face_send, face_recv, sp_send, sp_recv, mv_send, mv_recv, out_sem) = rest[24:]

    me = lax.axis_index("gx") * row + lax.axis_index("gy")
    core = lax.rem(me, 2)

    def device(d):
        d = lax.rem(d + devices, devices)
        return (d // row, lax.rem(d, row))

    peer = device(me + 1 - 2 * core)

    loads = [
        pltpu.make_async_copy(
            fields.at[:, :, :, pl.ds(q * 128, 128)], F.at[:, :, pl.ds(q * 32, 32), :], in_sem.at[q]
        )
        for q in range(8)
    ] + [
        pltpu.make_async_copy(
            speeds.at[:, :, :, pl.ds(q * 128, 128)],
            S.at[:, :, pl.ds(q * 32, 32), :],
            in_sem.at[8 + q],
        )
        for q in range(8)
    ]
    for load in loads:
        load.start()

    barrier = pltpu.get_barrier_semaphore()
    for offset in (-2, -1, 1, 2):
        pl.semaphore_signal(barrier, inc=1, device_id=device(me + offset), device_id_type=MESH)
    pl.semaphore_wait(barrier, 4)

    def remote(src, dst, send, recv, target):
        return pltpu.make_async_remote_copy(
            src_ref=src, dst_ref=dst, send_sem=send, recv_sem=recv,
            device_id=target, device_id_type=MESH,
        )

    class Exchange:
        def __init__(self, slot_at, send, recv):
            self.at, self.send, self.recv = slot_at, send, recv

        def start(self):
            own = self.at(2)
            self.far_up = remote(own, self.at(0), self.send.at[0], self.recv.at[0], device(me + 2))
            self.far_down = remote(
                own, self.at(4), self.send.at[1], self.recv.at[4], device(me - 2)
            )
            near = 1 + 2 * core
            self.near = remote(own, self.at(near), self.send.at[2], self.recv.at[near], peer)
            self.far_up.start()
            self.far_down.start()
            self.near.start()

        def forward(self):
            self.got(0)
            self.got(4)
            source, target = 4 - 4 * core, 3 - 2 * core
            self.passed = remote(
                self.at(source), self.at(target), self.send.at[3], self.recv.at[target], peer
            )
            self.passed.start()

        def got(self, slot):
            remote(
                self.at(slot), self.at(slot), self.send.at[0], self.recv.at[slot], peer
            ).wait_recv()

        def finish(self):
            self.got(1)
            self.got(3)

        def sent(self):
            for copy in (self.far_up, self.far_down, self.near, self.passed):
                copy.wait_send()

    def pairs(pool):
        return lambda slot: pool.at[pl.ds(2 * slot, 2)]

    def single(pool):
        return lambda slot: pool.at[slot]

    faces = [
        [
            Exchange(
                single(pools[s][f]) if s == 1 else pairs(pools[s][f]),
                face_send.at[s, f],
                face_recv.at[s, f],
            )
            for f in range(NF)
        ]
        for s in range(3)
    ]
    winds = [
        Exchange(at, sp_send.at[s], sp_recv.at[s])
        for s, at in enumerate((pairs(SP0), single(SP1), pairs(SP2)))
    ]

    sub = lax.broadcasted_iota(jnp.int32, (8, 128), 0)
    lane = lax.broadcasted_iota(jnp.int32, (8, 128), 1)

    def spot(b, d, h):
        return sel[b * 6 + 2 * d + h]

    def linked(b, d, h):
        return sel[12 + b * 6 + 2 * d + h]

    def pack_rows(s, f, A):
        pool = pools[s][f]
        for b in range(NB):
            for m in range(3):
                pool[4 + b, m] = A[b, f, pl.ds(m, 8, stride=32), :]
                pool[4 + b, 3 + m] = A[b, f, pl.ds(29 + m, 8, stride=32), :]

    def shift_up(x, ghost):
        return jnp.where(sub == 7, ghost, pltpu.roll(x, 7, 0))

    def shift_down(x, ghost):
        return jnp.where(sub == 0, ghost, pltpu.roll(x, 1, 0))

    def coef_rows(A, index, SP, d, C):
        def step(it, carry):
            b, c = it // 8, lax.rem(it, 8)
            base = c * 32
            own = [A[b, index, pl.ds(base + r, 8, stride=4), :] for r in range(4)]
            edge = A[b, index, pl.ds(base + 31, 1), :]
            ghost = SP[spot(b, d, 1), pl.ds(c, 1), :]
            ghost = chosen(linked(b, d, 1), (1, 128), ghost, edge)
            for r, value in enumerate(own + [shift_up(own[0], ghost)]):
                for n, part in enumerate(coefficients(value)):
                    C[it, 3 * r + n] = part
            return carry

        lax.fori_loop(0, 16, step, 0)

    def sweep_rows(s, f, A, C, strided):
        pool = pools[s][f]

        def step(it, carry):
            b, c = it // 8, lax.rem(it, 8)
            base = pl.multiple_of(c * 32, 32)
            own = [A[b, f, pl.ds(base + r, 8, stride=4), :] for r in range(4)]
            low_edge = A[b, f, pl.ds(base, 1), :]
            high_edge = A[b, f, pl.ds(base + 31, 1), :]
            low, high = spot(b, s, 0), spot(b, s, 1)
            low_on, high_on = linked(b, s, 0), linked(b, s, 1)
            before, after = [], []
            for m in range(3):
                ghost = chosen(low_on, (1, 128), pool[low, 3 + m, pl.ds(c, 1), :], low_edge)
                before.append(shift_down(own[m + 1], ghost))
                ghost = chosen(high_on, (1, 128), pool[high, m, pl.ds(c, 1), :], high_edge)
                after.append(shift_up(own[m], ghost))
            courant = [[C[it, 3 * r + n] for n in range(3)] for r in range(5)]
            result = ppm(before + own + after, courant)
            for r in range(4):
                if strided:
                    A[b, f, pl.ds(base + r, 8, stride=4), :] = result[r]
                else:
                    A[b, f, pl.ds(base + 8 * r, 8), :] = result[r]
            return carry

        lax.fori_loop(0, 16, step, 0)

    def side_up(x, ghost):
        return [
            pltpu.roll(jnp.where(lane < 32, x[1], x[0]), 96, 1),
            pltpu.roll(jnp.where(lane < 32, ghost, x[1]), 96, 1),
        ]

    def side_down(x, ghost):
        return [
            pltpu.roll(jnp.where(lane >= 96, ghost, x[0]), 32, 1),
            pltpu.roll(jnp.where(lane >= 96, x[0], x[1]), 32, 1),
        ]

    def pack_side(f):
        pool = pools[1][f]

        def step(o, carry):
            at = pl.multiple_of(o * 8, 8)
            for m in range(3):
                low = [T[b, f, pl.ds(m * 32 + at, 8), :] for b in range(NB)]
                high = [T[b, f, pl.ds(128 + (m + 1) * 32 + at, 8), :] for b in range(NB)]
                pool[2, m, pl.ds(at, 8), :] = jnp.where(
                    lane < 64,
                    jnp.where(lane < 32, low[0], pltpu.roll(low[1], 32, 1)),
                    jnp.where(lane >= 96, high[0], pltpu.roll(high[1], 96, 1)),
                )
            return carry

        lax.fori_loop(0, 4, step, 0)

    def coef_side():
        def step(it, carry):
            b, o = it // 4, lax.rem(it, 4)
            at = pl.multiple_of(o * 8, 8)
            own = [
                [ST[b, 0, pl.ds(h * 128 + g * 32 + at, 8), :] for h in range(2)] for g in range(4)
            ]
            where = spot(b, 1, 1)
            ghost = SP1[where // 2, pl.ds(at, 8), :]
            ghost = chosen(lax.rem(where, 2), (8, 128), pltpu.roll(ghost, 96, 1), ghost)
            ghost = chosen(linked(b, 1, 1), (8, 128), ghost, pltpu.roll(own[3][1], 32, 1))
            for r, value in enumerate(own + [side_up(own[0], ghost)]):
                for h in range(2):
                    for n, part in enumerate(coefficients(value[h])):
                        C1[it * 2 + h, 3 * r + n] = part
            return carry

        lax.fori_loop(0, 8, step, 0)

    def sweep_side(f):
        pool = pools[1][f]

        def step(it, carry):
            b, o = it // 4, lax.rem(it, 4)
            at = pl.multiple_of(o * 8, 8)
            own = [
                [T[b, f, pl.ds(h * 128 + g * 32 + at, 8), :] for h in range(2)] for g in range(4)
            ]
            low_edge = pltpu.roll(own[0][0], 96, 1)
            high_edge = pltpu.roll(own[3][1], 32, 1)
            low, high = spot(b, 1, 0), spot(b, 1, 1)
            low_on, high_on = linked(b, 1, 0), linked(b, 1, 1)
            before, after = [], []
            for m in range(3):
                ghost = pool[low // 2, m, pl.ds(at, 8), :]
                ghost = chosen(lax.rem(low, 2), (8, 128), pltpu.roll(ghost, 32, 1), ghost)
                ghost = chosen(low_on, (8, 128), ghost, low_edge)
                before.append(side_down(own[m + 1], ghost))
                ghost = pool[high // 2, m, pl.ds(at, 8), :]
                ghost = chosen(lax.rem(high, 2), (8, 128), pltpu.roll(ghost, 96, 1), ghost)
                ghost = chosen(high_on, (8, 128), ghost, high_edge)
                after.append(side_up(own[m], ghost))
            cells = before + own + after
            for h in range(2):
                courant = [[C1[it * 2 + h, 3 * r + n] for n in range(3)] for r in range(5)]
                result = ppm([x[h] for x in cells], courant)
                for g in range(4):
                    T[b, f, pl.ds(h * 128 + g * 32 + at, 8), :] = result[g]
            return carry

        lax.fori_loop(0, 8, step, 0)

    def turn(f):
        def step(it, carry):
            b, at = it // 2, pl.multiple_of(lax.rem(it, 2) * 128, 128)
            T[b, f, pl.ds(at, 128), :] = F[b, f, pl.ds(at, 128), :].T
            return carry

        lax.fori_loop(0, 4, step, 0)

    def turn_speeds():
        for n in range(2):
            def step(it, carry):
                b, h = it // 2, lax.rem(it, 2)
                rows = [
                    S[b, n + 1, pl.ds(h * 128 + q * 32 + r, 8, stride=4), :]
                    for q in range(4)
                    for r in range(4)
                ]
                at = pl.multiple_of(h * 128, 128)
                ST[b, n, pl.ds(at, 128), :] = jnp.concatenate(rows, axis=0).T
                return carry

            lax.fori_loop(0, 4, step, 0)

    def turn_back(f):
        def step(it, carry):
            b, h = it // 2, lax.rem(it, 2)
            back = T[b, f, pl.ds(pl.multiple_of(h * 128, 128), 128), :].T
            for q in range(4):
                for r in range(4):
                    R[f][2 + b, pl.ds(h * 128 + q * 32 + r, 8, stride=4), :] = back[
                        q * 32 + r * 8 : q * 32 + r * 8 + 8
                    ]
            return carry

        lax.fori_loop(0, 4, step, 0)

    for load in loads:
        load.wait()
    for b in range(NB):
        SP0[4 + b] = S[b, 0, pl.ds(0, 8, stride=32), :]
    winds[0].start()
    for f in range(NF):
        pack_rows(0, f, F)
        faces[0][f].start()
    turn_speeds()
    for b in range(NB):
        SP2[4 + b] = ST[b, 1, pl.ds(0, 8, stride=32), :]
    for o in range(4):
        at = o * 8
        SP1[2, pl.ds(at, 8), :] = jnp.where(
            lane < 32,
            ST[0, 0, pl.ds(at, 8), :],
            pltpu.roll(ST[1, 0, pl.ds(at, 8), :], 32, 1),
        )
    winds[1].start()
    winds[2].start()
    winds[0].forward()
    faces[0][0].forward()
    winds[0].finish()
    coef_rows(S, 0, SP0, 0, C0)

    moves = []
    for t in range(3 * NF):
        s, f = t // NF, t % NF
        if t + 1 < 3 * NF:
            faces[(t + 1) // NF][(t + 1) % NF].forward()
        if t == 1:
            winds[1].forward()
            winds[2].forward()
        if t == 4:
            winds[1].finish()
            winds[2].finish()
            coef_side()
            coef_rows(ST, 1, SP2, 2, C2)
        faces[s][f].finish()
        if s == 0:
            sweep_rows(0, f, F, C0, False)
            turn(f)
            pack_side(f)
            faces[1][f].start()
        elif s == 1:
            sweep_side(f)
            pack_rows(2, f, T)
            faces[2][f].start()
        else:
            sweep_rows(2, f, T, C2, True)
            turn_back(f)
            own = R[f].at[pl.ds(2, 2)]
            pair = [
                remote(own, R[f].at[pl.ds(0, 2)], mv_send.at[f, 0], mv_recv.at[f, 0], device(me + 1)),
                remote(own, R[f].at[pl.ds(4, 2)], mv_send.at[f, 1], mv_recv.at[f, 1], device(me - 1)),
            ]
            for copy in pair:
                copy.start()
            moves.append(pair)

    stores = []
    for f in range(NF):
        for copy in moves[f]:
            copy.wait_recv()
        for j in range(NB):
            def step(i, carry):
                at = pl.multiple_of(i * 8, 8)
                for q in range(8):
                    O[j, f, pl.ds(at, 8), pl.ds(q * 128, 128)] = R[f][
                        sel[24 + j], pl.ds(q * 32 + at, 8), :
                    ]
                return carry

            lax.fori_loop(0, 4, step, 0)
        stores.append(pltpu.make_async_copy(O.at[:, f], out.at[:, f], out_sem.at[f]))
        stores[-1].start()
    for group in faces + [winds]:
        for exchange in group:
            exchange.sent()
    for pair in moves:
        for copy in pair:
            copy.wait_send()
    for store in stores:
        store.wait()


def advance(fields, speeds, sel, devices, row):
    f32 = jnp.float32
    dma = pltpu.SemaphoreType.DMA
    scratch = [
        pltpu.VMEM((NB, NF, 256, 128), f32),
        pltpu.VMEM((NB, 3, 256, 128), f32),
        pltpu.VMEM((NB, NF, 256, 128), f32),
        pltpu.VMEM((NB, 2, 256, 128), f32),
        pltpu.VMEM((NB, NF, 32, 1024), f32),
        pltpu.VMEM((10, 8, 128), f32),
        pltpu.VMEM((5, 32, 128), f32),
        pltpu.VMEM((10, 8, 128), f32),
    ]
    scratch += [pltpu.VMEM((16, 15, 8, 128), f32) for _ in range(3)]
    for s in range(3):
        shape = (5, 3, 32, 128) if s == 1 else (10, 6, 8, 128)
        scratch += [pltpu.VMEM(shape, f32) for _ in range(NF)]
    scratch += [pltpu.VMEM((6, 256, 128), f32) for _ in range(NF)]
    scratch += [
        dma((16,)), dma((3, NF, 4)), dma((3, NF, 5)), dma((3, 4)), dma((3, 5)),
        dma((NF, 2)), dma((NF, 2)), dma((NF,)),
    ]
    return pl.pallas_call(
        functools.partial(advance_kernel, devices, row),
        out_shape=jax.ShapeDtypeStruct(fields.shape, f32),
        in_specs=[
            pl.BlockSpec(memory_space=pltpu.SMEM),
            pl.BlockSpec(memory_space=pl.ANY),
            pl.BlockSpec(memory_space=pl.ANY),
        ],
        out_specs=pl.BlockSpec(memory_space=pl.ANY),
        scratch_shapes=scratch,
        name="advance_blocks",
        compiler_params=pltpu.CompilerParams(
            collective_id=0, has_side_effects=True, vmem_limit_bytes=40 * 1024 * 1024
        ),
    )(sel, fields, speeds)


def body(fields, speeds, neighbours, block_order, tiles, tile_fill, tile_dest):
    row = lax.axis_size("gy")
    devices = lax.axis_size(AXES)
    me = lax.axis_index(AXES)
    first_block = me * NB

    target = tile_dest[:, 0]
    meta = jnp.stack([target, tile_fill])
    everyone = lax.all_gather(meta, AXES)

    links = lax.dynamic_slice_in_dim(neighbours, first_block, NB).reshape(-1)
    spots = jnp.clip((links // 2 - me + 2) * 2 + links % 2, 0, 9)
    incoming = lax.dynamic_slice_in_dim(block_order, first_block, NB)
    picks = jnp.clip((incoming // 2 - me + 1) * 2 + incoming % 2, 0, 5)
    sel = jnp.concatenate([spots, (links >= 0).astype(jnp.int32), picks])

    match = target[None, :] == jnp.arange(devices, dtype=jnp.int32)[:, None]
    inverse, fills = first_two(match, tile_fill[None, :])
    outgoing = pack_tiles(tiles, inverse, fills, devices * CAPT)
    tiles_out = lax.all_to_all(outgoing, AXES, split_axis=0, concat_axis=0, tiled=True)

    blocks_out = advance(fields, speeds, sel, devices, row)
    _, fill_out = first_two(everyone[:, 0] == me, everyone[:, 1])
    return blocks_out, tiles_out, fill_out


def solution(mesh):
    blocks = P(AXES, None, None, None)
    return jax.shard_map(
        body,
        mesh=mesh,
        in_specs=(blocks, blocks, P(), P(), P(AXES, None, None), P(AXES), P(AXES, None)),
        out_specs=(blocks, P(AXES, None, None), P(AXES)),
        check_vma=False,
    )
```

time: 379 us -> 126 us (0.33)
  the two profiles are of different devices: /device:TPU:112 before, /device:TPU:0 now
where the time goes in v1:
time: 126 us; the launch traced here: 124 us
  Pallas kernels  69.7 us (55%)
  blocking collectives  32.5 us (26%)
  starting transfers between devices  11.7 us (9%)
  local copies, waits for them, and re-layouts  7.39 us (6%)
  other arithmetic  2.13 us (2%)
    pallas_call x1, Pallas kernels, advance(): pl.pallas_call(functools.partial(advance_kernel, devices, row), out_shape...  66.9 us
    all_gather x1, blocking collectives, body(): everyone = lax.all_gather(meta, AXES)  32.5 us
    all_to_all x1, starting transfers between devices, body(): lax.all_to_all(outgoing, AXES, split_axis=0, concat_axis=0, tiled=True)  11.7 us
    unnamed x14, local copies, waits for them, and re-layouts  4.56 us
    pallas_call x1, Pallas kernels, pack_tiles(): pl.pallas_call(pack_kernel, out_shape=jax.ShapeDtypeStruct((slots,) + til...  2.78 us
  transfers between devices with their start and end apart: 1, of which 0 were waited for; matrix products, arithmetic and copies ran while one was open for 1% of the time, Pallas kernels for 54%

profile of v1, /device:TPU:0, one launch (start us, length us, event | category | flops | bytes accessed | tf_op | source)
XLA Modules:
  0.0 124.2 jit_solution(10236470070372579486)
XLA Ops:
  0.6 0.0 copy-start
  0.6 0.8 select_reduce_fusion.7
  1.5 0.1 copy.16
  1.6 0.7 min.30.inverse
  2.3 0.8 select_reduce_fusion.5
  3.1 0.1 copy.17
  3.2 0.7 reshape.45.fills
  4.0 0.0 copy-start.5
  4.0 0.0 copy-start.1
  4.0 2.8 %pack_tiles.1 = f32[256,8,128]{2,1,0:T(8,128)} custom-call(s32[256]{0:T(256)} %min.30.inverse, s32[256]{0:T(256)} %reshape.45.fills, f32[128,8,128]{2,1,0:T(8,128)} %tiles.1), custom_call_target="tpu_custom_call" | custom-call | tf_op jit(solution)/shard_map/pack_tiles/pallas_call | solution.py:34
  6.7 11.7 %all-to-all-start = ((f32[256,8,128]{2,1,0:T(8,128)}), f32[256,8,128]{2,1,0:T(8,128)}, u32[]{:S(2)}, u32[]{:S(2)}) async-start(f32[256,8,128]{2,1,0:T(8,128)} %pack_tiles.1), calls=%async_computation | async-start | bytes 2097152 | tf_op jit(solution)/shard_map/all_to_all | solution.py:526
  18.4 0.0 copy-done
  18.4 0.1 constant_dynamic-slice_fusion
  18.5 0.1 copy.15
  18.6 0.1 reshape.44
  18.7 0.0 copy-done.5
  18.7 0.1 fusion.2
  18.8 0.1 pad_add_fusion.2.sel
  18.9 0.0 copy-done.1
  18.9 0.0 copy-start.2
  18.9 1.1 copy-done.2
  20.0 0.0 copy-start.3
  20.0 0.0 copy-start.4
  20.0 66.9 %advance_blocks.1 = f32[2,6,32,1024]{3,2,1,0:T(8,128)S(1)} custom-call(s32[26]{0:T(128)S(1)} %pad_add_fusion.2.sel, f32[2,6,32,1024]{3,2,1,0:T(8,128)S(1)} %copy-done.1, f32[2,3,32,1024]{3,2,1,0:T(8,128)S(1)} %copy-done.2), custom_call_target="tpu_custom_call" | custom-call | tf_op jit(solution)/shard_map/advance_blocks/pallas_call | solution.py:490
  87.0 0.0 copy-done.3
  87.0 0.0 copy-done.4
  87.0 32.5 %all-gather.1 = s32[128,2,128]{2,1,0:T(2,128)S(1)} all-gather(s32[1,2,128]{2,1,0:T(2,128)S(1)} %add_bitcast_fusion), channel_id=2, replica_groups=mesh['gx'=4,'gy'=32] {'gx','gy'}, dimensions={0}, use_global_device_ids=true | all-gather | bytes 132096 | tf_op jit(solution)/shard_map/all_gather | solution.py:515
  119.5 0.1 fusion.4
  119.6 0.1 select_reduce_fusion.3
  119.7 0.2 select_reduce_fusion.2
  119.9 0.1 copy.19
  120.0 0.7 reshape.46
  120.7 0.0 all-to-all-done
  120.7 1.1 copy.23
  121.9 2.3 %copy.24 = f32[256,8,128]{2,1,0:T(8,128)} copy(f32[256,8,128]{2,1,0:T(8,128)} %all-to-all-done) | data formatting | bytes 2097152
  (9 shorter events, 0.1 us)
Async XLA Ops:
  0.6 17.8 %copy-start = (s32[256,6]{0,1:T(8,128)S(1)}, s32[256,6]{0,1:T(8,128)}, u32[]{:S(2)}) copy-start(s32[256,6]{0,1:T(8,128)} %param.9) | copy-start | bytes 18436
  4.0 14.8 %copy-start.5 = (s32[256]{0:T(256)S(1)}, s32[256]{0:T(256)}, u32[]{:S(2)}) copy-start(s32[256]{0:T(256)} %param.10) | copy-start | bytes 3076
  4.0 14.9 %copy-start.1 = (f32[2,6,32,1024]{3,2,1,0:T(8,128)S(1)}, f32[2,6,32,1024]{3,2,1,0:T(8,128)}, u32[]{:S(2)}) copy-start(f32[2,6,32,1024]{3,2,1,0:T(8,128)} %fields.1) | copy-start | bytes 4718596
  6.7 114.0 %all-to-all-start = ((f32[256,8,128]{2,1,0:T(8,128)}), f32[256,8,128]{2,1,0:T(8,128)}, u32[]{:S(2)}, u32[]{:S(2)}) async-start(f32[256,8,128]{2,1,0:T(8,128)} %pack_tiles.1), calls=%async_computation | async-start | bytes 2097152 | tf_op jit(solution)/shard_map/all_to_all | solution.py:526
  18.9 1.1 copy-start.2
  20.0 66.9 %copy-start.3 = (s32[128]{0:T(128)S(1)}, s32[128]{0:T(128)}, u32[]{:S(2)}) copy-start(s32[128]{0:T(128)} %param.12) | copy-start | bytes 1540
  20.0 67.0 %copy-start.4 = (s32[128,1]{0,1:T(1,128)S(1)}, s32[128,1]{0,1:T(1,128)}, u32[]{:S(2)}) copy-start(s32[128,1]{0,1:T(1,128)} %param.13) | copy-start | bytes 1540

commit v2 on v1

--- a/solution.py
+++ b/solution.py
@@ -13,47 +13,6 @@
 CAPT = 2
 DRIFT = 0.5
 AXES = ("gx", "gy")
-
-
-def pack_kernel(inverse, fills, tiles, out):
-    lane = lax.broadcasted_iota(jnp.int32, (3, 128), 1)
-    lane5 = lax.broadcasted_iota(jnp.int32, (5, 128), 1)
-
-    def step(slot, carry):
-        tile = inverse[slot]
-        fill = fills[slot]
-        head = tiles[tile, 0:3] + DRIFT * tiles[tile, 3:6]
-        out[slot, 0:3] = jnp.where(lane < fill, head, 0.0)
-        out[slot, 3:8] = jnp.where(lane5 < fill, tiles[tile, 3:8], 0.0)
-        return carry
-
-    lax.fori_loop(0, out.shape[0], step, 0, unroll=8)
-
-
-def pack_tiles(tiles, inverse, fills, slots):
-    return pl.pallas_call(
-        pack_kernel,
-        out_shape=jax.ShapeDtypeStruct((slots,) + tiles.shape[1:], tiles.dtype),
-        in_specs=[
-            pl.BlockSpec(memory_space=pltpu.SMEM),
-            pl.BlockSpec(memory_space=pltpu.SMEM),
-            pl.BlockSpec(memory_space=pltpu.VMEM),
-        ],
-        out_specs=pl.BlockSpec(memory_space=pltpu.VMEM),
-        name="pack_tiles",
-    )(inverse, fills, tiles)
-
-
-def first_two(match, fill):
-    width = match.shape[1]
-    index = lax.broadcasted_iota(jnp.int32, match.shape, 1)
-    first = jnp.min(jnp.where(match, index, width), axis=1)
-    last = jnp.max(jnp.where(match, index, -1), axis=1)
-    first_fill = jnp.sum(jnp.where(index == first[:, None], fill, 0), axis=1)
-    second = jnp.where(last > first, last, width)
-    second_fill = jnp.sum(jnp.where(index == second[:, None], fill, 0), axis=1)
-    where = jnp.stack([first, second], axis=1).reshape(-1)
-    return jnp.minimum(where, width - 1), jnp.stack([first_fill, second_fill], axis=1).reshape(-1)
 
 
 def ppm(cells, courant):
@@ -95,14 +54,51 @@
     return jnp.where(jnp.full(shape, flag, jnp.int32) != 0, ghost, edge)
 
 
-def advance_kernel(devices, row, sel, fields, speeds, out, *scratch):
-    (F, S, T, ST, O, SP0, SP1, SP2, C0, C1, C2), rest = scratch[:11], scratch[11:]
+def tree(op, x):
+    parts = [x[8 * i : 8 * i + 8] for i in range(16)]
+    while len(parts) > 1:
+        parts = [op(p, q) for p, q in zip(parts[::2], parts[1::2])]
+    value = parts[0]
+    for shift in (4, 2, 1):
+        value = op(value, pltpu.roll(value, shift, 0))
+    return value
+
+
+FILL_AT = (3, 5, 7, 9)
+RING_AT = 4
+LAST_AT = (8, 10)
+ORDER = sorted(((s, f) for s in range(3) for f in range(NF)), key=lambda t: (2 * t[1] + 6 * t[0], -t[0]))
+
+
+def advance_kernel(devices, row, sel, fields, speeds, tiles, dest, fill, *refs):
+    out, tiles_out, fill_out = refs[:3]
+    (F, S, T, ST, O, SP0, SP1, SP2, C0, C1, C2), rest = refs[3:14], refs[14:]
     pools = [rest[6 * s : 6 * s + 6] for s in range(3)]
-    R = rest[18:24]
-    (in_sem, face_send, face_recv, sp_send, sp_recv, mv_send, mv_recv, out_sem) = rest[24:]
-
-    me = lax.axis_index("gx") * row + lax.axis_index("gy")
-    core = lax.rem(me, 2)
+    R, rest = rest[18:24], rest[24:]
+    (TL, G, INV, INVS), B0, B1, B2, rest = rest[:4], rest[4:6], rest[6:8], rest[8:10], rest[10:]
+    (in_sem, face_send, face_recv, sp_send, sp_recv, mv_send, mv_recv, out_sem) = rest[:8]
+    (inv_sem, ring_send, ring_recv, own_sem, last_send, last_recv, all_send, all_recv) = rest[8:]
+
+    gx, gy = lax.axis_index("gx"), lax.axis_index("gy")
+    me = gx * row + gy
+    core = lax.rem(gy, 2)
+    gz, yc, y = gy // 8, lax.rem(gy, 8), lax.rem(gy // 2, 4)
+
+    def along_x(k):
+        x = lax.rem(gx + k, 4)
+        return x, (x, gy)
+
+    def along_z(k):
+        z = lax.rem(gz + k, 4)
+        return z, (gx, z * 8 + yc)
+
+    def along_yc(k):
+        n = lax.rem(yc + k, 8)
+        return n, (gx, gz * 8 + n)
+
+    def along_y(k):
+        n = lax.rem(y + k, 4)
+        return n, (gx, gz * 8 + n * 2 + core)
 
     def device(d):
         d = lax.rem(d + devices, devices)
@@ -123,13 +119,17 @@
         )
         for q in range(8)
     ]
-    for load in loads:
+    tile_load = pltpu.make_async_copy(tiles, TL, in_sem.at[16])
+    for load in loads + [tile_load]:
         load.start()
 
     barrier = pltpu.get_barrier_semaphore()
-    for offset in (-2, -1, 1, 2):
-        pl.semaphore_signal(barrier, inc=1, device_id=device(me + offset), device_id_type=MESH)
-    pl.semaphore_wait(barrier, 4)
+    greeted = [device(me + offset) for offset in (-2, -1, 1, 2)]
+    greeted += [along_x(k)[1] for k in (1, 2, 3)] + [along_z(k)[1] for k in (1, 2, 3)]
+    greeted += [along_yc(k)[1] for k in range(1, 8)]
+    for other in greeted:
+        pl.semaphore_signal(barrier, inc=1, device_id=other, device_id_type=MESH)
+    pl.semaphore_wait(barrier, len(greeted))
 
     def remote(src, dst, send, recv, target):
         return pltpu.make_async_remote_copy(
@@ -260,7 +260,7 @@
                     A[b, f, pl.ds(base + 8 * r, 8), :] = result[r]
             return carry
 
-        lax.fori_loop(0, 16, step, 0)
+        lax.fori_loop(0, 16, step, 0, unroll=4)
 
     def side_up(x, ghost):
         return [
@@ -341,7 +341,7 @@
                     T[b, f, pl.ds(h * 128 + g * 32 + at, 8), :] = result[g]
             return carry
 
-        lax.fori_loop(0, 8, step, 0)
+        lax.fori_loop(0, 8, step, 0, unroll=2)
 
     def turn(f):
         def step(it, carry):
@@ -349,7 +349,7 @@
             T[b, f, pl.ds(at, 128), :] = F[b, f, pl.ds(at, 128), :].T
             return carry
 
-        lax.fori_loop(0, 4, step, 0)
+        lax.fori_loop(0, 4, step, 0, unroll=4)
 
     def turn_speeds():
         for n in range(2):
@@ -377,7 +377,151 @@
                     ]
             return carry
 
-        lax.fori_loop(0, 4, step, 0)
+        lax.fori_loop(0, 4, step, 0, unroll=4)
+
+    def find_tiles():
+        t = lax.broadcasted_iota(jnp.int32, (128, 128), 0)
+        p = lax.broadcasted_iota(jnp.int32, (128, 128), 1)
+        dests = jnp.broadcast_to(dest[...], (128, 128)).T
+        fills = jnp.broadcast_to(fill[...], (128, 128)).T
+        match = dests == p
+
+        def rows(x):
+            return jnp.concatenate([x] * 16, axis=0)
+
+        first = tree(jnp.minimum, jnp.where(match, t, 128))
+        last = tree(jnp.maximum, jnp.where(match, t, -1))
+        second = jnp.where(last > first, last, 128)
+        first_fill = tree(jnp.add, jnp.where(t == rows(first), fills, 0))
+        second_fill = tree(jnp.add, jnp.where(t == rows(second), fills, 0))
+        where = jnp.where(sub == 0, jnp.minimum(first, 127), jnp.minimum(second, 127))
+        INV[...] = jnp.where(sub < 2, where, jnp.where(sub == 2, first_fill, second_fill))
+        G[me, 0:1] = first_fill[0:1]
+        G[me, 1:2] = second_fill[0:1]
+        copy = pltpu.make_async_copy(INV, INVS, inv_sem)
+        copy.start()
+        return copy
+
+    def pack_tiles():
+        def step(i, carry):
+            for n in range(8):
+                for h in range(CAPT):
+                    x = TL[INVS[h, i * 8 + n]]
+                    moved = jnp.where(sub < 3, x + DRIFT * pltpu.roll(x, 5, 0), x)
+                    live = lane < jnp.full((8, 128), INVS[2 + h, i * 8 + n], jnp.int32)
+                    B0[h][i // 4, lax.rem(i, 4), n] = jnp.where(live, moved, 0.0)
+            return carry
+
+        lax.fori_loop(0, 16, step, 0)
+
+    def at_x(ref, n):
+        return ref.at[n]
+
+    def at_z(ref, n):
+        return ref.at[:, n]
+
+    class Ring:
+        def __init__(self, h, turn):
+            source, target = ((B0, B1), (B1, B2))[turn]
+            x_now = h == turn
+            along, at, here = (along_x, at_x, gx) if x_now else (along_z, at_z, gz)
+            self.own = pltpu.make_async_copy(
+                at(source[h], here), at(target[h], here), own_sem.at[h, turn]
+            )
+            self.copies, self.arrivals = [], []
+            for k in (1, 2, 3):
+                n, other = along(k)
+                send, recv = ring_send.at[h, turn, k], ring_recv.at[h, turn, k]
+                self.copies.append(
+                    remote(at(source[h], n), at(target[h], here), send, recv, other)
+                )
+                n, other = along(4 - k)
+                self.arrivals.append(
+                    remote(at(source[h], n), at(target[h], n), send, recv, other)
+                )
+
+        def start(self):
+            for copy in self.copies:
+                copy.start()
+            self.own.start()
+
+        def finish(self):
+            self.own.wait()
+            for copy in self.arrivals:
+                copy.wait_recv()
+
+        def sent(self):
+            for copy in self.copies:
+                copy.wait_send()
+
+    class Last:
+        def __init__(self, h):
+            self.own = pltpu.make_async_copy(
+                B2[h].at[:, :, yc], tiles_out.at[:, :, yc, h], own_sem.at[h, 2]
+            )
+            self.copies, self.arrivals = [], []
+            for k in range(1, 8):
+                send, recv = last_send.at[h, k], last_recv.at[h, k]
+                n, other = along_yc(k)
+                self.copies.append(
+                    remote(B2[h].at[:, :, n], tiles_out.at[:, :, yc, h], send, recv, other)
+                )
+                n, other = along_yc(8 - k)
+                self.arrivals.append(
+                    remote(B2[h].at[:, :, n], tiles_out.at[:, :, n, h], send, recv, other)
+                )
+
+        start, finish, sent = Ring.start, Ring.finish, Ring.sent
+
+    class Fills:
+        def __init__(self, n):
+            size = (1, 2, 8, 32)[n]
+            base = me // size * size
+            mine = G.at[pl.ds(base, size)]
+            self.copies, self.arrivals = [], []
+            for k in (1,) if n == 0 else (1, 2, 3):
+                send, recv = all_send.at[n, k], all_recv.at[n, k]
+                for list_, j in ((self.copies, k), (self.arrivals, (2 if n == 0 else 4) - k)):
+                    if n == 0:
+                        other, start = peer, me + 1 - 2 * core
+                    else:
+                        at, other = (along_y, along_z, along_x)[n - 1](j)
+                        start = base + (at - (y, gz, gx)[n - 1]) * size
+                    where = mine if list_ is self.copies else G.at[pl.ds(start, size)]
+                    list_.append(remote(mine, where, send, recv, other))
+
+        def start(self):
+            for copy in self.copies:
+                copy.start()
+
+        def finish(self):
+            for copy in self.arrivals:
+                copy.wait_recv()
+
+        sent = Ring.sent
+
+    rings = [[Ring(h, turn) for turn in range(2)] for h in range(CAPT)]
+    lasts = [Last(h) for h in range(CAPT)]
+    fill_steps = [Fills(n) for n in range(4)]
+
+    def own_fills():
+        flat = lax.broadcasted_iota(jnp.int32, (2, 128), 0) * 128
+        flat = flat + lax.broadcasted_iota(jnp.int32, (2, 128), 1)
+        mine = lax.broadcasted_iota(jnp.int32, (2, 128), 1) == me
+
+        def step(i, total):
+            for n in range(8):
+                source = i * 8 + n
+                value = jnp.sum(jnp.where(mine, G[source], 0), axis=1, keepdims=True)
+                for h in range(CAPT):
+                    total = jnp.where(
+                        flat == source * CAPT + h,
+                        jnp.broadcast_to(value[h : h + 1], (2, 128)),
+                        total,
+                    )
+            return total
+
+        fill_out[...] = lax.fori_loop(0, 16, step, jnp.zeros((2, 128), jnp.int32))
 
     for load in loads:
         load.wait()
@@ -387,7 +531,14 @@
     for f in range(NF):
         pack_rows(0, f, F)
         faces[0][f].start()
+    found = find_tiles()
+    fill_steps[0].start()
     turn_speeds()
+    found.wait()
+    tile_load.wait()
+    pack_tiles()
+    for h in range(CAPT):
+        rings[h][0].start()
     for b in range(NB):
         SP2[4 + b] = ST[b, 1, pl.ds(0, 8, stride=32), :]
     for o in range(4):
@@ -404,19 +555,37 @@
     winds[0].finish()
     coef_rows(S, 0, SP0, 0, C0)
 
-    moves = []
+    moves = {}
+    first_of = {s: min(t for t in range(3 * NF) if ORDER[t][0] == s) for s in range(3)}
     for t in range(3 * NF):
-        s, f = t // NF, t % NF
+        s, f = ORDER[t]
         if t + 1 < 3 * NF:
-            faces[(t + 1) // NF][(t + 1) % NF].forward()
+            after_s, after_f = ORDER[t + 1]
+            faces[after_s][after_f].forward()
         if t == 1:
             winds[1].forward()
             winds[2].forward()
-        if t == 4:
+        if t == first_of[1]:
             winds[1].finish()
+            coef_side()
+        if t == first_of[2]:
             winds[2].finish()
-            coef_side()
             coef_rows(ST, 1, SP2, 2, C2)
+        if t in FILL_AT:
+            n = FILL_AT.index(t)
+            fill_steps[n].finish()
+            if n < 3:
+                fill_steps[n + 1].start()
+            else:
+                own_fills()
+        if t == RING_AT:
+            for h in range(CAPT):
+                rings[h][0].finish()
+                rings[h][1].start()
+        if t in LAST_AT:
+            h = LAST_AT.index(t)
+            rings[h][1].finish()
+            lasts[h].start()
         faces[s][f].finish()
         if s == 0:
             sweep_rows(0, f, F, C0, False)
@@ -437,7 +606,7 @@
             ]
             for copy in pair:
                 copy.start()
-            moves.append(pair)
+            moves[f] = pair
 
     stores = []
     for f in range(NF):
@@ -455,18 +624,20 @@
             lax.fori_loop(0, 4, step, 0)
         stores.append(pltpu.make_async_copy(O.at[:, f], out.at[:, f], out_sem.at[f]))
         stores[-1].start()
-    for group in faces + [winds]:
+    for last in lasts:
+        last.finish()
+    for group in faces + [winds, fill_steps, lasts] + rings:
         for exchange in group:
             exchange.sent()
-    for pair in moves:
+    for pair in moves.values():
         for copy in pair:
             copy.wait_send()
     for store in stores:
         store.wait()
 
 
-def advance(fields, speeds, sel, devices, row):
-    f32 = jnp.float32
+def advance(fields, speeds, sel, tiles, dest, fill, devices, row):
+    f32, i32 = jnp.float32, jnp.int32
     dma = pltpu.SemaphoreType.DMA
     scratch = [
         pltpu.VMEM((NB, NF, 256, 128), f32),
@@ -484,24 +655,44 @@
         scratch += [pltpu.VMEM(shape, f32) for _ in range(NF)]
     scratch += [pltpu.VMEM((6, 256, 128), f32) for _ in range(NF)]
     scratch += [
-        dma((16,)), dma((3, NF, 4)), dma((3, NF, 5)), dma((3, 4)), dma((3, 5)),
+        pltpu.VMEM((128, 8, 128), f32),
+        pltpu.VMEM((128, CAPT, 128), i32),
+        pltpu.VMEM((8, 128), i32),
+        pltpu.SMEM((8, 128), i32),
+    ]
+    scratch += [pltpu.VMEM((4, 4, 8, 8, 128), f32) for _ in range(3 * CAPT)]
+    scratch += [
+        dma((17,)), dma((3, NF, 4)), dma((3, NF, 5)), dma((3, 4)), dma((3, 5)),
         dma((NF, 2)), dma((NF, 2)), dma((NF,)),
+        dma(()), dma((CAPT, 2, 4)), dma((CAPT, 2, 4)), dma((CAPT, 3)),
+        dma((CAPT, 8)), dma((CAPT, 8)), dma((4, 4)), dma((4, 4)),
     ]
     return pl.pallas_call(
         functools.partial(advance_kernel, devices, row),
-        out_shape=jax.ShapeDtypeStruct(fields.shape, f32),
+        out_shape=(
+            jax.ShapeDtypeStruct(fields.shape, f32),
+            jax.ShapeDtypeStruct((4, 4, 8, CAPT, 8, 128), f32),
+            jax.ShapeDtypeStruct((CAPT, 128), i32),
+        ),
         in_specs=[
             pl.BlockSpec(memory_space=pltpu.SMEM),
+            pl.BlockSpec(memory_space=pltpu.HBM),
+            pl.BlockSpec(memory_space=pltpu.HBM),
+            pl.BlockSpec(memory_space=pltpu.HBM),
+            pl.BlockSpec(memory_space=pltpu.VMEM),
+            pl.BlockSpec(memory_space=pltpu.VMEM),
+        ],
+        out_specs=(
             pl.BlockSpec(memory_space=pl.ANY),
             pl.BlockSpec(memory_space=pl.ANY),
-        ],
-        out_specs=pl.BlockSpec(memory_space=pl.ANY),
+            pl.BlockSpec(memory_space=pltpu.VMEM),
+        ),
         scratch_shapes=scratch,
         name="advance_blocks",
         compiler_params=pltpu.CompilerParams(
             collective_id=0, has_side_effects=True, vmem_limit_bytes=40 * 1024 * 1024
         ),
-    )(sel, fields, speeds)
+    )(sel, fields, speeds, tiles, dest, fill)
 
 
 def body(fields, speeds, neighbours, block_order, tiles, tile_fill, tile_dest):
@@ -510,24 +701,16 @@
     me = lax.axis_index(AXES)
     first_block = me * NB
 
-    target = tile_dest[:, 0]
-    meta = jnp.stack([target, tile_fill])
-    everyone = lax.all_gather(meta, AXES)
-
     links = lax.dynamic_slice_in_dim(neighbours, first_block, NB).reshape(-1)
     spots = jnp.clip((links // 2 - me + 2) * 2 + links % 2, 0, 9)
     incoming = lax.dynamic_slice_in_dim(block_order, first_block, NB)
     picks = jnp.clip((incoming // 2 - me + 1) * 2 + incoming % 2, 0, 5)
     sel = jnp.concatenate([spots, (links >= 0).astype(jnp.int32), picks])
 
-    match = target[None, :] == jnp.arange(devices, dtype=jnp.int32)[:, None]
-    inverse, fills = first_two(match, tile_fill[None, :])
-    outgoing = pack_tiles(tiles, inverse, fills, devices * CAPT)
-    tiles_out = lax.all_to_all(outgoing, AXES, split_axis=0, concat_axis=0, tiled=True)
-
-    blocks_out = advance(fields, speeds, sel, devices, row)
-    _, fill_out = first_two(everyone[:, 0] == me, everyone[:, 1])
-    return blocks_out, tiles_out, fill_out
+    blocks_out, tiles_out, fill_out = advance(
+        fields, speeds, sel, tiles, tile_dest.reshape(1, -1), tile_fill.reshape(1, -1), devices, row
+    )
+    return blocks_out, tiles_out.reshape((-1,) + tiles.shape[1:]), fill_out.reshape(-1)
 
 
 def solution(mesh):

time: 126 us -> 89.7 us (0.71); the launches traced: 124 us -> 89.4 us
  blocking collectives: 32.5 us -> 0 us
  starting transfers between devices: 11.7 us -> 0 us
  Pallas kernels: 69.7 us -> 80 us
    all_gather x1 -> x0, blocking collectives: 32.5 us -> none  [body(): everyone = lax.all_gather(meta, AXES)]
    pallas_call x1, Pallas kernels: 66.9 us -> 80 us  [advance(): pl.pallas_call(functools.partial(advance_kernel, devices, row), out_shape...]
    all_to_all x1 -> x0, starting transfers between devices: 11.7 us -> none  [body(): lax.all_to_all(outgoing, AXES, split_axis=0, concat_axis=0, tiled=True)]
    unnamed x14 -> x15, local copies, waits for them, and re-layouts: 4.56 us -> 7.58 us
    pallas_call x1 -> x0, Pallas kernels: 2.78 us -> none  [pack_tiles(): pl.pallas_call(pack_kernel, out_shape=jax.ShapeDtypeStruct((slots,) + til...]
    reshape x2 -> x0, local copies, waits for them, and re-layouts: 1.42 us -> none  [first_two(): jnp.stack([first_fill, second_fill], axis=1).reshape(-1)]
  transfers between devices with their start and end apart: 1 -> 0, of which waited for: 0 -> 0; matrix products, arithmetic and copies ran while one was open for 1% -> 0% of each run, Pallas kernels for 54% -> 0%
where the time goes in v2:
time: 89.7 us; the launch traced here: 89.4 us
  Pallas kernels  80 us (89%)
  local copies, waits for them, and re-layouts  7.84 us (9%)
    pallas_call x1, Pallas kernels, advance(): pl.pallas_call(functools.partial(advance_kernel, devices, row), out_shape...  80 us
    unnamed x15, local copies, waits for them, and re-layouts  7.58 us

profile of v2, /device:TPU:0, one launch (start us, length us, event | category | flops | bytes accessed | tf_op | source)
XLA Modules:
  0.0 89.4 jit_solution(13471934687007847537)
XLA Ops:
  0.6 0.0 copy-start
  0.7 0.8 fusion.2
  1.4 0.0 copy-done
  1.4 0.1 constant_dynamic-slice_fusion
  1.5 0.1 copy.10
  1.6 0.1 reshape.21
  1.7 0.1 pad_add_fusion.sel
  1.8 0.0 copy-start.1
  1.8 1.4 %copy-done.1 = f32[2,6,32,1024]{3,2,1,0:T(8,128)S(1)} copy-done((f32[2,6,32,1024]{3,2,1,0:T(8,128)S(1)}, f32[2,6,32,1024]{3,2,1,0:T(8,128)}, u32[]{:S(2)}) %copy-start.1) | copy-done | bytes 1572888
  3.2 0.0 copy-start.2
  3.2 1.1 %copy-done.2 = f32[2,3,32,1024]{3,2,1,0:T(8,128)S(1)} copy-done((f32[2,3,32,1024]{3,2,1,0:T(8,128)S(1)}, f32[2,3,32,1024]{3,2,1,0:T(8,128)}, u32[]{:S(2)}) %copy-start.2) | copy-done | bytes 786456
  4.3 0.0 copy-start.3
  4.3 1.0 %copy-done.3 = f32[128,8,128]{2,1,0:T(8,128)S(1)} copy-done((f32[128,8,128]{2,1,0:T(8,128)S(1)}, f32[128,8,128]{2,1,0:T(8,128)}, u32[]{:S(2)}) %copy-start.3) | copy-done | bytes 524312
  5.4 0.0 copy-start.4
  5.4 0.7 copy-done.4
  6.0 0.0 copy-start.5
  6.0 0.7 copy-done.5
  6.7 80.0 %advance_blocks.1 = (f32[2,6,32,1024]{3,2,1,0:T(8,128)S(1)}, f32[4,4,8,2,8,128]{5,4,3,2,1,0:T(8,128)S(1)}, s32[2,128]{1,0:T(2,128)S(1)}) custom-call(s32[26]{0:T(128)S(1)} %pad_add_fusion.sel, f32[2,6,32,1024]{3,2,1,0:T(8,128)S(1)} %copy-done.1, f32[2,3,32,1024]{3,2,1,0:T(8,128)S(1)} %copy-done.2, f32[128,8,128]{2,1,0:T(8,128)S(1)} %copy-done.3, ...), custom_call_target="tpu_custom_call" | custom-call | tf_op jit(solution)/shard_map/advance_blocks/pallas_call | solution.py:670
  86.7 1.1 %copy.14 = f32[2,6,32,1024]{3,2,1,0:T(8,128)} copy(f32[2,6,32,1024]{3,2,1,0:T(8,128)S(1)} %get-tuple-element.12) | data formatting | bytes 3145728
  87.9 1.0 %copy.15 = f32[256,8,128]{2,1,0:T(8,128)} copy(f32[256,8,128]{2,1,0:T(8,128)S(1)} %bitcast.4) | data formatting | bytes 2097152
  88.8 0.6 copy.16
  (2 shorter events, 0.0 us)
Async XLA Ops:
  0.6 0.8 copy-start
  1.8 1.4 %copy-start.1 = (f32[2,6,32,1024]{3,2,1,0:T(8,128)S(1)}, f32[2,6,32,1024]{3,2,1,0:T(8,128)}, u32[]{:S(2)}) copy-start(f32[2,6,32,1024]{3,2,1,0:T(8,128)} %fields.1) | copy-start | bytes 4718596
  3.2 1.1 %copy-start.2 = (f32[2,3,32,1024]{3,2,1,0:T(8,128)S(1)}, f32[2,3,32,1024]{3,2,1,0:T(8,128)}, u32[]{:S(2)}) copy-start(f32[2,3,32,1024]{3,2,1,0:T(8,128)} %speeds.1) | copy-start | bytes 2359300
  4.3 1.0 %copy-start.3 = (f32[128,8,128]{2,1,0:T(8,128)S(1)}, f32[128,8,128]{2,1,0:T(8,128)}, u32[]{:S(2)}) copy-start(f32[128,8,128]{2,1,0:T(8,128)} %tiles.1) | copy-start | bytes 1572868
  5.4 0.7 copy-start.4
  6.0 0.7 copy-start.5

commit v3 on v2

--- a/solution.py
+++ b/solution.py
@@ -16,22 +16,23 @@
 
 
 def ppm(cells, courant):
-    delta = [cells[i + 1] - cells[i] for i in range(9)]
+    n = len(cells) - 6
+    delta = [cells[i + 1] - cells[i] for i in range(n + 5)]
     right, left = {}, {}
-    for i in range(1, 8):
+    for i in range(1, n + 4):
         step = 0.5 * delta[i] + (1.0 / 12.0) * (delta[i - 1] - delta[i + 1])
         step = jnp.minimum(
             jnp.maximum(step, jnp.minimum(delta[i], 0.0)), jnp.maximum(delta[i], 0.0)
         )
         right[i], left[i + 1] = step, delta[i] - step
     up, down = {}, {}
-    for i in range(2, 8):
+    for i in range(2, n + 4):
         r, l = right[i], left[i]
         r2, l2 = r + r, l + l
         up[i] = jnp.maximum(jnp.minimum(r, l2), 0.0) + jnp.minimum(jnp.maximum(r, l2), 0.0)
         down[i] = jnp.maximum(jnp.minimum(l, r2), 0.0) + jnp.minimum(jnp.maximum(l, r2), 0.0)
     flux = []
-    for f in range(5):
+    for f in range(n + 1):
         c, ca, cb = courant[f]
         a, b = f + 2, f + 3
         wind = c > 0.0
@@ -40,7 +41,7 @@
             + ca * jnp.where(wind, up[a], down[b])
             + cb * jnp.where(wind, down[a], up[b])
         )
-    return [cells[r + 3] - (flux[r + 1] - flux[r]) for r in range(4)]
+    return [cells[r + 3] - (flux[r + 1] - flux[r]) for r in range(n)]
 
 
 def coefficients(c):
@@ -64,10 +65,10 @@
     return value
 
 
-FILL_AT = (3, 5, 7, 9)
-RING_AT = 4
-LAST_AT = (8, 10)
-ORDER = sorted(((s, f) for s in range(3) for f in range(NF)), key=lambda t: (2 * t[1] + 6 * t[0], -t[0]))
+FILL_AT = (2, 7, 12)
+PHASE_AT = ((8, 15), (8, 15))
+TILES_A_STEP = 3
+ORDER = [(s, f) for s in range(3) for f in range(NF)]
 
 
 def advance_kernel(devices, row, sel, fields, speeds, tiles, dest, fill, *refs):
@@ -77,7 +78,7 @@
     R, rest = rest[18:24], rest[24:]
     (TL, G, INV, INVS), B0, B1, B2, rest = rest[:4], rest[4:6], rest[6:8], rest[8:10], rest[10:]
     (in_sem, face_send, face_recv, sp_send, sp_recv, mv_send, mv_recv, out_sem) = rest[:8]
-    (inv_sem, ring_send, ring_recv, own_sem, last_send, last_recv, all_send, all_recv) = rest[8:]
+    (inv_sem, tile_send, tile_recv, own_sem, all_send, all_recv) = rest[8:]
 
     gx, gy = lax.axis_index("gx"), lax.axis_index("gy")
     me = gx * row + gy
@@ -232,7 +233,7 @@
                     C[it, 3 * r + n] = part
             return carry
 
-        lax.fori_loop(0, 16, step, 0)
+        lax.fori_loop(0, 16, step, 0, unroll=2)
 
     def sweep_rows(s, f, A, C, strided):
         pool = pools[s][f]
@@ -262,23 +263,10 @@
 
         lax.fori_loop(0, 16, step, 0, unroll=4)
 
-    def side_up(x, ghost):
-        return [
-            pltpu.roll(jnp.where(lane < 32, x[1], x[0]), 96, 1),
-            pltpu.roll(jnp.where(lane < 32, ghost, x[1]), 96, 1),
-        ]
-
-    def side_down(x, ghost):
-        return [
-            pltpu.roll(jnp.where(lane >= 96, ghost, x[0]), 32, 1),
-            pltpu.roll(jnp.where(lane >= 96, x[0], x[1]), 32, 1),
-        ]
-
     def pack_side(f):
         pool = pools[1][f]
-
-        def step(o, carry):
-            at = pl.multiple_of(o * 8, 8)
+        for o in range(4):
+            at = o * 8
             for m in range(3):
                 low = [T[b, f, pl.ds(m * 32 + at, 8), :] for b in range(NB)]
                 high = [T[b, f, pl.ds(128 + (m + 1) * 32 + at, 8), :] for b in range(NB)]
@@ -287,28 +275,31 @@
                     jnp.where(lane < 32, low[0], pltpu.roll(low[1], 32, 1)),
                     jnp.where(lane >= 96, high[0], pltpu.roll(high[1], 96, 1)),
                 )
-            return carry
-
-        lax.fori_loop(0, 4, step, 0)
+
+    def side_rows(A, b, n, at):
+        return [A[b, n, pl.ds(r * 32 + at, 8), :] for r in range(8)]
+
+    def before_first(ghost, second):
+        return chosen(second, (8, 128), pltpu.roll(ghost, 64, 1), pltpu.roll(ghost, 32, 1))
+
+    def after_last(ghost, second):
+        return chosen(second, (8, 128), pltpu.roll(ghost, 64, 1), pltpu.roll(ghost, 96, 1))
 
     def coef_side():
         def step(it, carry):
             b, o = it // 4, lax.rem(it, 4)
             at = pl.multiple_of(o * 8, 8)
-            own = [
-                [ST[b, 0, pl.ds(h * 128 + g * 32 + at, 8), :] for h in range(2)] for g in range(4)
-            ]
+            own = side_rows(ST, b, 0, at)
             where = spot(b, 1, 1)
-            ghost = SP1[where // 2, pl.ds(at, 8), :]
-            ghost = chosen(lax.rem(where, 2), (8, 128), pltpu.roll(ghost, 96, 1), ghost)
-            ghost = chosen(linked(b, 1, 1), (8, 128), ghost, pltpu.roll(own[3][1], 32, 1))
-            for r, value in enumerate(own + [side_up(own[0], ghost)]):
-                for h in range(2):
-                    for n, part in enumerate(coefficients(value[h])):
-                        C1[it * 2 + h, 3 * r + n] = part
+            ghost = after_last(SP1[where // 2, pl.ds(at, 8), :], lax.rem(where, 2))
+            ghost = chosen(linked(b, 1, 1), (8, 128), ghost, own[7])
+            own.append(jnp.where(lane >= 96, ghost, pltpu.roll(own[0], 96, 1)))
+            for r, value in enumerate(own):
+                for n, part in enumerate(coefficients(value)):
+                    C1[it, 3 * r + n] = part
             return carry
 
-        lax.fori_loop(0, 8, step, 0)
+        lax.fori_loop(0, 8, step, 0, unroll=2)
 
     def sweep_side(f):
         pool = pools[1][f]
@@ -316,37 +307,30 @@
         def step(it, carry):
             b, o = it // 4, lax.rem(it, 4)
             at = pl.multiple_of(o * 8, 8)
-            own = [
-                [T[b, f, pl.ds(h * 128 + g * 32 + at, 8), :] for h in range(2)] for g in range(4)
-            ]
-            low_edge = pltpu.roll(own[0][0], 96, 1)
-            high_edge = pltpu.roll(own[3][1], 32, 1)
+            own = side_rows(T, b, f, at)
             low, high = spot(b, 1, 0), spot(b, 1, 1)
             low_on, high_on = linked(b, 1, 0), linked(b, 1, 1)
             before, after = [], []
             for m in range(3):
-                ghost = pool[low // 2, m, pl.ds(at, 8), :]
-                ghost = chosen(lax.rem(low, 2), (8, 128), pltpu.roll(ghost, 32, 1), ghost)
-                ghost = chosen(low_on, (8, 128), ghost, low_edge)
-                before.append(side_down(own[m + 1], ghost))
-                ghost = pool[high // 2, m, pl.ds(at, 8), :]
-                ghost = chosen(lax.rem(high, 2), (8, 128), pltpu.roll(ghost, 96, 1), ghost)
-                ghost = chosen(high_on, (8, 128), ghost, high_edge)
-                after.append(side_up(own[m], ghost))
-            cells = before + own + after
-            for h in range(2):
-                courant = [[C1[it * 2 + h, 3 * r + n] for n in range(3)] for r in range(5)]
-                result = ppm([x[h] for x in cells], courant)
-                for g in range(4):
-                    T[b, f, pl.ds(h * 128 + g * 32 + at, 8), :] = result[g]
+                ghost = before_first(pool[low // 2, m, pl.ds(at, 8), :], lax.rem(low, 2))
+                ghost = chosen(low_on, (8, 128), ghost, own[0])
+                before.append(jnp.where(lane < 32, ghost, pltpu.roll(own[5 + m], 32, 1)))
+                ghost = after_last(pool[high // 2, m, pl.ds(at, 8), :], lax.rem(high, 2))
+                ghost = chosen(high_on, (8, 128), ghost, own[7])
+                after.append(jnp.where(lane >= 96, ghost, pltpu.roll(own[m], 96, 1)))
+            courant = [[C1[it, 3 * r + n] for n in range(3)] for r in range(9)]
+            result = ppm(before + own + after, courant)
+            for r in range(8):
+                T[b, f, pl.ds(r * 32 + at, 8), :] = result[r]
             return carry
 
         lax.fori_loop(0, 8, step, 0, unroll=2)
 
     def turn(f):
         def step(it, carry):
-            b, at = it // 2, pl.multiple_of(lax.rem(it, 2) * 128, 128)
-            T[b, f, pl.ds(at, 128), :] = F[b, f, pl.ds(at, 128), :].T
+            b, e = it // 2, lax.rem(it, 2)
+            rows = [F[b, f, pl.ds((2 * q + e) * 32, 32), :] for q in range(4)]
+            T[b, f, pl.ds(e * 128, 128), :] = jnp.concatenate(rows, axis=0).T
             return carry
 
         lax.fori_loop(0, 4, step, 0, unroll=4)
@@ -354,25 +338,24 @@
     def turn_speeds():
         for n in range(2):
             def step(it, carry):
-                b, h = it // 2, lax.rem(it, 2)
+                b, e = it // 2, lax.rem(it, 2)
                 rows = [
-                    S[b, n + 1, pl.ds(h * 128 + q * 32 + r, 8, stride=4), :]
+                    S[b, n + 1, pl.ds((2 * q + e) * 32 + r, 8, stride=4), :]
                     for q in range(4)
                     for r in range(4)
                 ]
-                at = pl.multiple_of(h * 128, 128)
-                ST[b, n, pl.ds(at, 128), :] = jnp.concatenate(rows, axis=0).T
+                ST[b, n, pl.ds(e * 128, 128), :] = jnp.concatenate(rows, axis=0).T
                 return carry
 
-            lax.fori_loop(0, 4, step, 0)
+            lax.fori_loop(0, 4, step, 0, unroll=4)
 
     def turn_back(f):
         def step(it, carry):
-            b, h = it // 2, lax.rem(it, 2)
-            back = T[b, f, pl.ds(pl.multiple_of(h * 128, 128), 128), :].T
+            b, e = it // 2, lax.rem(it, 2)
+            back = T[b, f, pl.ds(pl.multiple_of(e * 128, 128), 128), :].T
             for q in range(4):
                 for r in range(4):
-                    R[f][2 + b, pl.ds(h * 128 + q * 32 + r, 8, stride=4), :] = back[
+                    R[f][2 + b, pl.ds((2 * q + e) * 32 + r, 8, stride=4), :] = back[
                         q * 32 + r * 8 : q * 32 + r * 8 + 8
                     ]
             return carry
@@ -414,31 +397,16 @@
 
         lax.fori_loop(0, 16, step, 0)
 
-    def at_x(ref, n):
-        return ref.at[n]
-
-    def at_z(ref, n):
-        return ref.at[:, n]
-
-    class Ring:
-        def __init__(self, h, turn):
-            source, target = ((B0, B1), (B1, B2))[turn]
-            x_now = h == turn
-            along, at, here = (along_x, at_x, gx) if x_now else (along_z, at_z, gz)
-            self.own = pltpu.make_async_copy(
-                at(source[h], here), at(target[h], here), own_sem.at[h, turn]
-            )
+    class Part:
+        def __init__(self, size, along, source, target, send, recv, own):
+            here = along(0)[0]
+            self.own = pltpu.make_async_copy(source(here), target(here), own)
             self.copies, self.arrivals = [], []
-            for k in (1, 2, 3):
+            for k in range(1, size):
                 n, other = along(k)
-                send, recv = ring_send.at[h, turn, k], ring_recv.at[h, turn, k]
-                self.copies.append(
-                    remote(at(source[h], n), at(target[h], here), send, recv, other)
-                )
-                n, other = along(4 - k)
-                self.arrivals.append(
-                    remote(at(source[h], n), at(target[h], n), send, recv, other)
-                )
+                self.copies.append(remote(source(n), target(here), send.at[k], recv.at[k], other))
+                n, other = along(size - k)
+                self.arrivals.append(remote(source(n), target(n), send.at[k], recv.at[k], other))
 
         def start(self):
             for copy in self.copies:
@@ -454,24 +422,20 @@
             for copy in self.copies:
                 copy.wait_send()
 
-    class Last:
-        def __init__(self, h):
-            self.own = pltpu.make_async_copy(
-                B2[h].at[:, :, yc], tiles_out.at[:, :, yc, h], own_sem.at[h, 2]
-            )
-            self.copies, self.arrivals = [], []
-            for k in range(1, 8):
-                send, recv = last_send.at[h, k], last_recv.at[h, k]
-                n, other = along_yc(k)
-                self.copies.append(
-                    remote(B2[h].at[:, :, n], tiles_out.at[:, :, yc, h], send, recv, other)
-                )
-                n, other = along_yc(8 - k)
-                self.arrivals.append(
-                    remote(B2[h].at[:, :, n], tiles_out.at[:, :, n, h], send, recv, other)
-                )
-
-        start, finish, sent = Ring.start, Ring.finish, Ring.sent
+    def seen(ref, axis, n, *half):
+        after = (slice(None),) * (2 - axis) if half else ()
+        return ref.at[(slice(None),) * axis + (n,) + after + half]
+
+    def part(h, phase):
+        axis = ((2, 0, 1), (1, 0, 2))[h][phase]
+        size, along = (4, 4, 8)[axis], (along_x, along_z, along_yc)[axis]
+        source = (B0, B1, B2)[phase][h]
+        target, half = (tiles_out, (h,)) if phase == 2 else ((B1, B2)[phase][h], ())
+        return Part(
+            size, along,
+            lambda n: seen(source, axis, n), lambda n: seen(target, axis, n, *half),
+            tile_send.at[h, phase], tile_recv.at[h, phase], own_sem.at[h, phase],
+        )
 
     class Fills:
         def __init__(self, n):
@@ -498,10 +462,9 @@
             for copy in self.arrivals:
                 copy.wait_recv()
 
-        sent = Ring.sent
-
-    rings = [[Ring(h, turn) for turn in range(2)] for h in range(CAPT)]
-    lasts = [Last(h) for h in range(CAPT)]
+        sent = Part.sent
+
+    parts = [[part(h, phase) for phase in range(3)] for h in range(CAPT)]
     fill_steps = [Fills(n) for n in range(4)]
 
     def own_fills():
@@ -537,8 +500,19 @@
     found.wait()
     tile_load.wait()
     pack_tiles()
+    queue = list(parts[0][0].copies)
+    for n, copy in enumerate(parts[1][0].copies):
+        queue.insert(3 * n, copy)
     for h in range(CAPT):
-        rings[h][0].start()
+        parts[h][0].own.start()
+
+    def tiles_at(t):
+        for h in range(CAPT):
+            for phase in range(2):
+                if t == PHASE_AT[h][phase]:
+                    parts[h][phase].finish()
+                    parts[h][phase + 1].start()
+
     for b in range(NB):
         SP2[4 + b] = ST[b, 1, pl.ds(0, 8, stride=32), :]
     for o in range(4):
@@ -574,18 +548,8 @@
         if t in FILL_AT:
             n = FILL_AT.index(t)
             fill_steps[n].finish()
-            if n < 3:
-                fill_steps[n + 1].start()
-            else:
-                own_fills()
-        if t == RING_AT:
-            for h in range(CAPT):
-                rings[h][0].finish()
-                rings[h][1].start()
-        if t in LAST_AT:
-            h = LAST_AT.index(t)
-            rings[h][1].finish()
-            lasts[h].start()
+            fill_steps[n + 1].start()
+        tiles_at(t)
         faces[s][f].finish()
         if s == 0:
             sweep_rows(0, f, F, C0, False)
@@ -607,9 +571,15 @@
             for copy in pair:
                 copy.start()
             moves[f] = pair
-
+        for _ in range(TILES_A_STEP):
+            if queue:
+                queue.pop(0).start()
+
+    fill_steps[3].finish()
+    own_fills()
     stores = []
     for f in range(NF):
+        tiles_at(3 * NF + f)
         for copy in moves[f]:
             copy.wait_recv()
         for j in range(NB):
@@ -621,12 +591,12 @@
                     ]
                 return carry
 
-            lax.fori_loop(0, 4, step, 0)
+            lax.fori_loop(0, 4, step, 0, unroll=2)
         stores.append(pltpu.make_async_copy(O.at[:, f], out.at[:, f], out_sem.at[f]))
         stores[-1].start()
-    for last in lasts:
-        last.finish()
-    for group in faces + [winds, fill_steps, lasts] + rings:
+    for h in range(CAPT):
+        parts[h][2].finish()
+    for group in faces + [winds, fill_steps] + parts:
         for exchange in group:
             exchange.sent()
     for pair in moves.values():
@@ -649,7 +619,7 @@
         pltpu.VMEM((5, 32, 128), f32),
         pltpu.VMEM((10, 8, 128), f32),
     ]
-    scratch += [pltpu.VMEM((16, 15, 8, 128), f32) for _ in range(3)]
+    scratch += [pltpu.VMEM((8, 27, 8, 128) if s == 1 else (16, 15, 8, 128), f32) for s in range(3)]
     for s in range(3):
         shape = (5, 3, 32, 128) if s == 1 else (10, 6, 8, 128)
         scratch += [pltpu.VMEM(shape, f32) for _ in range(NF)]
@@ -664,8 +634,7 @@
     scratch += [
         dma((17,)), dma((3, NF, 4)), dma((3, NF, 5)), dma((3, 4)), dma((3, 5)),
         dma((NF, 2)), dma((NF, 2)), dma((NF,)),
-        dma(()), dma((CAPT, 2, 4)), dma((CAPT, 2, 4)), dma((CAPT, 3)),
-        dma((CAPT, 8)), dma((CAPT, 8)), dma((4, 4)), dma((4, 4)),
+        dma(()), dma((CAPT, 3, 8)), dma((CAPT, 3, 8)), dma((CAPT, 3)), dma((4, 4)), dma((4, 4)),
     ]
     return pl.pallas_call(
         functools.partial(advance_kernel, devices, row),
@@ -690,7 +659,7 @@
         scratch_shapes=scratch,
         name="advance_blocks",
         compiler_params=pltpu.CompilerParams(
-            collective_id=0, has_side_effects=True, vmem_limit_bytes=40 * 1024 * 1024
+            collective_id=0, has_side_effects=True, vmem_limit_bytes=60 * 1024 * 1024
         ),
     )(sel, fields, speeds, tiles, dest, fill)
 

time: 89.7 us -> 83.2 us (0.928)
  Pallas kernels: 80 us -> 76.3 us
  local copies, waits for them, and re-layouts: 7.84 us -> 4.63 us
    pallas_call x1, Pallas kernels: 80 us -> 76.3 us  [advance(): pl.pallas_call(functools.partial(advance_kernel, devices, row), out_shape...]
    unnamed x15 -> x9, local copies, waits for them, and re-layouts: 7.58 us -> 4.37 us
where the time goes in v3:
time: 83.2 us; the launch traced here: 83 us
  Pallas kernels  76.3 us (92%)
  local copies, waits for them, and re-layouts  4.63 us (6%)
  other arithmetic  1.38 us (2%)
    pallas_call x1, Pallas kernels, advance(): pl.pallas_call(functools.partial(advance_kernel, devices, row), out_shape...  76.3 us
    unnamed x9, local copies, waits for them, and re-layouts  4.37 us

profile of v3, /device:TPU:0, one launch (start us, length us, event | category | flops | bytes accessed | tf_op | source)
XLA Modules:
  0.0 83.0 jit_solution(4446587019782188555)
XLA Ops:
  0.6 0.0 copy-start
  0.7 0.8 fusion.2
  1.4 0.0 copy-done
  1.4 0.1 constant_dynamic-slice_fusion
  1.5 0.1 copy.10
  1.6 0.1 reshape.21
  1.7 0.6 pad_add_fusion.sel
  2.3 76.3 %advance_blocks.1 = (f32[2,6,32,1024]{3,2,1,0:T(8,128)}, f32[4,4,8,2,8,128]{5,4,3,2,1,0:T(8,128)}, s32[2,128]{1,0:T(2,128)}) custom-call(s32[26]{0:T(128)} %pad_add_fusion.sel, f32[2,6,32,1024]{3,2,1,0:T(8,128)} %fields.1, f32[2,3,32,1024]{3,2,1,0:T(8,128)} %speeds.1, f32[128,8,128]{2,1,0:T(8,128)} %tiles.1, s32[1,128]{1,0:T(1,128)} %bitcast.6, s32[1,128]{1,0:T(1,128)} %bitcast.7), custom_call_target="tpu_custom_call" | custom-call | tf_op jit(solution)/shard_map/advance_blocks/pallas_call | solution.py:639
  78.6 0.0 copy-start.1
  78.6 2.8 %copy.14 = f32[2,6,32,1024]{3,2,1,0:T(8,128)} copy(f32[2,6,32,1024]{3,2,1,0:T(8,128)} %get-tuple-element.12) | data formatting | bytes 3145728
  81.4 0.0 copy-done.1
  81.4 0.0 copy-start.2
  81.4 1.0 %copy.15 = f32[256,8,128]{2,1,0:T(8,128)} copy(f32[256,8,128]{2,1,0:T(8,128)S(1)} %bitcast.4) | data formatting | bytes 2097152
  82.4 0.0 copy-done.2
  82.4 0.6 copy.16
  (2 shorter events, 0.0 us)
Async XLA Ops:
  0.6 0.8 copy-start
  78.6 2.8 %copy-start.1 = (f32[4,4,8,2,8,128]{5,4,3,2,1,0:T(8,128)S(1)}, f32[4,4,8,2,8,128]{5,4,3,2,1,0:T(8,128)}, u32[]{:S(2)}) copy-start(f32[4,4,8,2,8,128]{5,4,3,2,1,0:T(8,128)} %get-tuple-element.7) | copy-start | bytes 3145732
  81.4 1.0 %copy-start.2 = (s32[2,128]{1,0:T(2,128)S(1)}, s32[2,128]{1,0:T(2,128)}, u32[]{:S(2)}) copy-start(s32[2,128]{1,0:T(2,128)} %get-tuple-element.8) | copy-start | bytes 3076

commit v4 on v3

--- a/solution.py
+++ b/solution.py
@@ -71,7 +71,7 @@
 ORDER = [(s, f) for s in range(3) for f in range(NF)]
 
 
-def advance_kernel(devices, row, sel, fields, speeds, tiles, dest, fill, *refs):
+def advance_kernel(devices, row, neighbours, order, fields, speeds, tiles, dest, fill, *refs):
     out, tiles_out, fill_out = refs[:3]
     (F, S, T, ST, O, SP0, SP1, SP2, C0, C1, C2), rest = refs[3:14], refs[14:]
     pools = [rest[6 * s : 6 * s + 6] for s in range(3)]
@@ -201,11 +201,15 @@
     sub = lax.broadcasted_iota(jnp.int32, (8, 128), 0)
     lane = lax.broadcasted_iota(jnp.int32, (8, 128), 1)
 
+    def place(n, reach):
+        found = (jnp.right_shift(n, 1) - me + reach) * 2 + jnp.bitwise_and(n, 1)
+        return jnp.minimum(jnp.maximum(found, 0), 4 * reach + 1)
+
     def spot(b, d, h):
-        return sel[b * 6 + 2 * d + h]
+        return place(neighbours[2 * d + h, me * NB + b], 2)
 
     def linked(b, d, h):
-        return sel[12 + b * 6 + 2 * d + h]
+        return (neighbours[2 * d + h, me * NB + b] >= 0).astype(jnp.int32)
 
     def pack_rows(s, f, A):
         pool = pools[s][f]
@@ -587,7 +591,7 @@
                 at = pl.multiple_of(i * 8, 8)
                 for q in range(8):
                     O[j, f, pl.ds(at, 8), pl.ds(q * 128, 128)] = R[f][
-                        sel[24 + j], pl.ds(q * 32 + at, 8), :
+                        place(order[me * NB + j], 1), pl.ds(q * 32 + at, 8), :
                     ]
                 return carry
 
@@ -606,7 +610,7 @@
         store.wait()
 
 
-def advance(fields, speeds, sel, tiles, dest, fill, devices, row):
+def advance(fields, speeds, neighbours, order, tiles, dest, fill, devices, row):
     f32, i32 = jnp.float32, jnp.int32
     dma = pltpu.SemaphoreType.DMA
     scratch = [
@@ -645,6 +649,7 @@
         ),
         in_specs=[
             pl.BlockSpec(memory_space=pltpu.SMEM),
+            pl.BlockSpec(memory_space=pltpu.SMEM),
             pl.BlockSpec(memory_space=pltpu.HBM),
             pl.BlockSpec(memory_space=pltpu.HBM),
             pl.BlockSpec(memory_space=pltpu.HBM),
@@ -661,23 +666,15 @@
         compiler_params=pltpu.CompilerParams(
             collective_id=0, has_side_effects=True, vmem_limit_bytes=60 * 1024 * 1024
         ),
-    )(sel, fields, speeds, tiles, dest, fill)
+    )(neighbours, order, fields, speeds, tiles, dest, fill)
 
 
 def body(fields, speeds, neighbours, block_order, tiles, tile_fill, tile_dest):
     row = lax.axis_size("gy")
     devices = lax.axis_size(AXES)
-    me = lax.axis_index(AXES)
-    first_block = me * NB
-
-    links = lax.dynamic_slice_in_dim(neighbours, first_block, NB).reshape(-1)
-    spots = jnp.clip((links // 2 - me + 2) * 2 + links % 2, 0, 9)
-    incoming = lax.dynamic_slice_in_dim(block_order, first_block, NB)
-    picks = jnp.clip((incoming // 2 - me + 1) * 2 + incoming % 2, 0, 5)
-    sel = jnp.concatenate([spots, (links >= 0).astype(jnp.int32), picks])
-
     blocks_out, tiles_out, fill_out = advance(
-        fields, speeds, sel, tiles, tile_dest.reshape(1, -1), tile_fill.reshape(1, -1), devices, row
+        fields, speeds, neighbours.T, block_order, tiles,
+        tile_dest.reshape(1, -1), tile_fill.reshape(1, -1), devices, row,
     )
     return blocks_out, tiles_out.reshape((-1,) + tiles.shape[1:]), fill_out.reshape(-1)
 

time: 83.2 us -> 81.9 us (0.984)
  other arithmetic: 1.38 us -> 0 us
    unnamed x9 -> x7, local copies, waits for them, and re-layouts: 4.37 us -> 4.36 us
where the time goes in v4:
time: 81.9 us; the launch traced here: 81.7 us
  Pallas kernels  76.7 us (94%)
  local copies, waits for them, and re-layouts  4.36 us (5%)
    pallas_call x1, Pallas kernels, advance(): pl.pallas_call(functools.partial(advance_kernel, devices, row), out_shape...  76.7 us
    unnamed x7, local copies, waits for them, and re-layouts  4.36 us

profile of v4, /device:TPU:0, one launch (start us, length us, event | category | flops | bytes accessed | tf_op | source)
XLA Modules:
  0.0 81.7 jit_solution(12211204328758977747)
XLA Ops:
  0.6 76.7 %advance_blocks.1 = (f32[2,6,32,1024]{3,2,1,0:T(8,128)}, f32[4,4,8,2,8,128]{5,4,3,2,1,0:T(8,128)}, s32[2,128]{1,0:T(2,128)}) custom-call(s32[6,256]{1,0:T(8,128)} %bitcast.6, s32[256]{0:T(256)} %order.1, f32[2,6,32,1024]{3,2,1,0:T(8,128)} %fields.1, f32[2,3,32,1024]{3,2,1,0:T(8,128)} %speeds.1, f32[128,8,128]{2,1,0:T(8,128)} %tiles.1, s32[1,128]{1,0:T(1,128)} %bitcast.8, ...), custom_call_target="tpu_custom_call" | custom-call | tf_op jit(solution)/shard_map/advance_blocks/pallas_call | solution.py:643
  77.4 0.0 copy-start
  77.4 2.8 %copy.13 = f32[2,6,32,1024]{3,2,1,0:T(8,128)} copy(f32[2,6,32,1024]{3,2,1,0:T(8,128)} %get-tuple-element.12) | data formatting | bytes 3145728
  80.2 0.0 copy-done
  80.2 0.0 copy-start.1
  80.2 1.0 %copy.14 = f32[256,8,128]{2,1,0:T(8,128)} copy(f32[256,8,128]{2,1,0:T(8,128)S(1)} %bitcast.5) | data formatting | bytes 2097152
  81.2 0.0 copy-done.1
  81.2 0.6 copy.15
Async XLA Ops:
  77.4 2.8 %copy-start = (f32[4,4,8,2,8,128]{5,4,3,2,1,0:T(8,128)S(1)}, f32[4,4,8,2,8,128]{5,4,3,2,1,0:T(8,128)}, u32[]{:S(2)}) copy-start(f32[4,4,8,2,8,128]{5,4,3,2,1,0:T(8,128)} %get-tuple-element.7) | copy-start | bytes 3145732
  80.2 1.0 %copy-start.1 = (s32[2,128]{1,0:T(2,128)S(1)}, s32[2,128]{1,0:T(2,128)}, u32[]{:S(2)}) copy-start(s32[2,128]{1,0:T(2,128)} %get-tuple-element.8) | copy-start | bytes 3076

commit v5 on v4

--- a/solution.py
+++ b/solution.py
@@ -431,7 +431,7 @@
         return ref.at[(slice(None),) * axis + (n,) + after + half]
 
     def part(h, phase):
-        axis = ((2, 0, 1), (1, 0, 2))[h][phase]
+        axis = ((0, 2, 1), (1, 0, 2))[h][phase]
         size, along = (4, 4, 8)[axis], (along_x, along_z, along_yc)[axis]
         source = (B0, B1, B2)[phase][h]
         target, half = (tiles_out, (h,)) if phase == 2 else ((B1, B2)[phase][h], ())

time: 81.9 us -> 80.5 us (0.983)
  Pallas kernels: 76.7 us -> 74.7 us
    pallas_call x1, Pallas kernels: 76.7 us -> 74.7 us  [advance(): pl.pallas_call(functools.partial(advance_kernel, devices, row), out_shape...]
where the time goes in v5:
time: 80.5 us; the launch traced here: 79.8 us
  Pallas kernels  74.7 us (93%)
  local copies, waits for them, and re-layouts  4.36 us (5%)
    pallas_call x1, Pallas kernels, advance(): pl.pallas_call(functools.partial(advance_kernel, devices, row), out_shape...  74.7 us
    unnamed x7, local copies, waits for them, and re-layouts  4.36 us

profile of v5, /device:TPU:0, one launch (start us, length us, event | category | flops | bytes accessed | tf_op | source)
XLA Modules:
  0.0 79.8 jit_solution(15928400219072645928)
XLA Ops:
  0.6 74.7 %advance_blocks.1 = (f32[2,6,32,1024]{3,2,1,0:T(8,128)}, f32[4,4,8,2,8,128]{5,4,3,2,1,0:T(8,128)}, s32[2,128]{1,0:T(2,128)}) custom-call(s32[6,256]{1,0:T(8,128)} %bitcast.6, s32[256]{0:T(256)} %order.1, f32[2,6,32,1024]{3,2,1,0:T(8,128)} %fields.1, f32[2,3,32,1024]{3,2,1,0:T(8,128)} %speeds.1, f32[128,8,128]{2,1,0:T(8,128)} %tiles.1, s32[1,128]{1,0:T(1,128)} %bitcast.8, ...), custom_call_target="tpu_custom_call" | custom-call | tf_op jit(solution)/shard_map/advance_blocks/pallas_call | solution.py:643
  75.4 0.0 copy-start
  75.4 2.8 %copy.13 = f32[2,6,32,1024]{3,2,1,0:T(8,128)} copy(f32[2,6,32,1024]{3,2,1,0:T(8,128)} %get-tuple-element.12) | data formatting | bytes 3145728
  78.2 0.0 copy-done
  78.2 0.0 copy-start.1
  78.2 1.0 %copy.14 = f32[256,8,128]{2,1,0:T(8,128)} copy(f32[256,8,128]{2,1,0:T(8,128)S(1)} %bitcast.5) | data formatting | bytes 2097152
  79.2 0.0 copy-done.1
  79.2 0.6 copy.15
Async XLA Ops:
  75.4 2.8 %copy-start = (f32[4,4,8,2,8,128]{5,4,3,2,1,0:T(8,128)S(1)}, f32[4,4,8,2,8,128]{5,4,3,2,1,0:T(8,128)}, u32[]{:S(2)}) copy-start(f32[4,4,8,2,8,128]{5,4,3,2,1,0:T(8,128)} %get-tuple-element.7) | copy-start | bytes 3145732
  78.2 1.0 %copy-start.1 = (s32[2,128]{1,0:T(2,128)S(1)}, s32[2,128]{1,0:T(2,128)}, u32[]{:S(2)}) copy-start(s32[2,128]{1,0:T(2,128)} %get-tuple-element.8) | copy-start | bytes 3076

commit v6 on v5

--- a/solution.py
+++ b/solution.py
@@ -155,9 +155,8 @@
             self.near.start()
 
         def forward(self):
-            self.got(0)
-            self.got(4)
             source, target = 4 - 4 * core, 3 - 2 * core
+            self.got(source)
             self.passed = remote(
                 self.at(source), self.at(target), self.send.at[3], self.recv.at[target], peer
             )
@@ -169,6 +168,7 @@
             ).wait_recv()
 
         def finish(self):
+            self.got(4 * core)
             self.got(1)
             self.got(3)
 

time: 80.5 us -> 81.1 us (level)
  no operation moved by 1% of the time
where the time goes in v6:
time: 81.1 us; the launch traced here: 80.1 us
  Pallas kernels  75.1 us (93%)
  local copies, waits for them, and re-layouts  4.36 us (5%)
    pallas_call x1, Pallas kernels, advance(): pl.pallas_call(functools.partial(advance_kernel, devices, row), out_shape...  75.1 us
    unnamed x7, local copies, waits for them, and re-layouts  4.36 us

profile of v6, /device:TPU:0, one launch (start us, length us, event | category | flops | bytes accessed | tf_op | source)
XLA Modules:
  0.0 80.1 jit_solution(11823033995162988940)
XLA Ops:
  0.6 75.1 %advance_blocks.1 = (f32[2,6,32,1024]{3,2,1,0:T(8,128)}, f32[4,4,8,2,8,128]{5,4,3,2,1,0:T(8,128)}, s32[2,128]{1,0:T(2,128)}) custom-call(s32[6,256]{1,0:T(8,128)} %bitcast.6, s32[256]{0:T(256)} %order.1, f32[2,6,32,1024]{3,2,1,0:T(8,128)} %fields.1, f32[2,3,32,1024]{3,2,1,0:T(8,128)} %speeds.1, f32[128,8,128]{2,1,0:T(8,128)} %tiles.1, s32[1,128]{1,0:T(1,128)} %bitcast.8, ...), custom_call_target="tpu_custom_call" | custom-call | tf_op jit(solution)/shard_map/advance_blocks/pallas_call | solution.py:643
  75.8 0.0 copy-start
  75.8 2.8 %copy.13 = f32[2,6,32,1024]{3,2,1,0:T(8,128)} copy(f32[2,6,32,1024]{3,2,1,0:T(8,128)} %get-tuple-element.12) | data formatting | bytes 3145728
  78.6 0.0 copy-done
  78.6 0.0 copy-start.1
  78.6 1.0 %copy.14 = f32[256,8,128]{2,1,0:T(8,128)} copy(f32[256,8,128]{2,1,0:T(8,128)S(1)} %bitcast.5) | data formatting | bytes 2097152
  79.6 0.0 copy-done.1
  79.6 0.6 copy.15
Async XLA Ops:
  75.8 2.8 %copy-start = (f32[4,4,8,2,8,128]{5,4,3,2,1,0:T(8,128)S(1)}, f32[4,4,8,2,8,128]{5,4,3,2,1,0:T(8,128)}, u32[]{:S(2)}) copy-start(f32[4,4,8,2,8,128]{5,4,3,2,1,0:T(8,128)} %get-tuple-element.7) | copy-start | bytes 3145732
  78.6 1.0 %copy-start.1 = (s32[2,128]{1,0:T(2,128)S(1)}, s32[2,128]{1,0:T(2,128)}, u32[]{:S(2)}) copy-start(s32[2,128]{1,0:T(2,128)} %get-tuple-element.8) | copy-start | bytes 3076
